TPU v7x, 256 devices: a whole 4x4x8 slice. The times are simulated.
256 devices in a mesh: gx: 8 (over z_lo, y), gy: 16 (over x, z_hi), row: 2 (over core).
Axes of the slice: x: 4, y: 4, z: 8 (z_hi: 4, z_lo: 2; z = z_hi * 2 + z_lo), core: 2. Of those that a mesh axis runs over, the one named last changes fastest.
Arguments:
- initial_velocity: float32 [16, 512, 4096], P('row', 'gx', 'gy'), may hold values from -6 to 6
- background_speed: float32 [512, 4096], P('gx', 'gy'), may hold values from 0.98 to 1
- density: float32 [512, 4096], P('gx', 'gy'), may hold values from 1.5 to 3
- east_modes: float32 [512, 96], P('gx', 'gy'), may hold values from -0.625 to 0.625
- north_modes: float32 [96, 4096], P('gx', 'gy'), may hold values from -0.625 to 0.625
- mode_coef: float32 [16, 96, 96], P('row', 'gy'), may hold values from -5 to 5
Outputs:
- peak_velocity: float32 [16, 512, 4096], P('row', 'gx', 'gy')
All inputs are finite; a program needn't handle non-finite values.
Results may differ from a plain program's by a relative error of at most 0.00011.
Values sent between devices are 32-bit elements; how exact they have to be, the bound alone decides.
A program may use at most 64 MiB of HBM per device.

v0:
```python
import jax
import jax.numpy as jnp
from jax import lax
from jax.sharding import PartitionSpec as P

STEPS = 6


coef_near = 9.0 / 8.0
coef_far = -1.0 / 24.0
time_step = 0.55
perturb_gain = 0.03


def extended(cells, sides, width):
    for axis, dim in sides:
        count = lax.axis_size(axis)
        ends = count - 1
        head = lax.slice_in_dim(cells, 0, width, axis=dim)
        tail = lax.slice_in_dim(cells, cells.shape[dim] - width, cells.shape[dim], axis=dim)
        cells = jnp.concatenate(
            [
                lax.ppermute(tail, axis, [(i, (i + 1) % count) for i in range(ends)]),
                cells,
                lax.ppermute(head, axis, [((i + 1) % count, i) for i in range(ends)]),
            ],
            axis=dim,
        )
    return cells


def on_device(initial_velocity, background_speed, density, east_modes, north_modes, mode_coef):
    reals, size_x, size_y = initial_velocity.shape
    panel = jnp.einsum(
        "xk,rkm->rxm",
        lax.all_gather(east_modes, "gy", axis=1, tiled=True),
        lax.all_gather(mode_coef, "gy", axis=1, tiled=True),
        precision=lax.Precision.HIGHEST,
        preferred_element_type=jnp.float32,
    )
    shape_field = jnp.einsum(
        "rxk,ky->rxy",
        panel,
        lax.all_gather(north_modes, "gx", axis=0, tiled=True),
        precision=lax.Precision.HIGHEST,
        preferred_element_type=jnp.float32,
    )
    speed = background_speed[None] * (1.0 + perturb_gain * jnp.tanh(shape_field))
    modulus = density[None] * speed * speed
    buoyancy = time_step / density
    velocity = initial_velocity
    peak = jnp.zeros_like(velocity)
    stress_east = jnp.zeros_like(velocity)
    stress_north = jnp.zeros_like(velocity)
    for step in range(STEPS):
        padded = extended(velocity, (("gx", 1), ("gy", 2)), 2)
        mid = padded[:, :, 2 : size_y + 2]
        grad_east = coef_near * (mid[:, 3 : size_x + 3] - mid[:, 2 : size_x + 2]) + coef_far * (
            mid[:, 4 : size_x + 4] - mid[:, 1 : size_x + 1]
        )
        mid = padded[:, 2 : size_x + 2, :]
        grad_north = coef_near * (
            mid[:, :, 3 : size_y + 3] - mid[:, :, 2 : size_y + 2]
        ) + coef_far * (mid[:, :, 4 : size_y + 4] - mid[:, :, 1 : size_y + 1])
        stress_east = stress_east + time_step * modulus * grad_east
        stress_north = stress_north + time_step * modulus * grad_north
        east_pad = extended(stress_east, (("gx", 1),), 2)
        north_pad = extended(stress_north, (("gy", 2),), 2)
        div_east = coef_near * (
            east_pad[:, 2 : size_x + 2] - east_pad[:, 1 : size_x + 1]
        ) + coef_far * (east_pad[:, 3 : size_x + 3] - east_pad[:, 0:size_x])
        div_north = coef_near * (
            north_pad[:, :, 2 : size_y + 2] - north_pad[:, :, 1 : size_y + 1]
        ) + coef_far * (north_pad[:, :, 3 : size_y + 3] - north_pad[:, :, 0:size_y])
        velocity = velocity + buoyancy[None] * (div_east + div_north)
        peak = jnp.maximum(peak, jnp.abs(velocity))
    return peak


def solution(mesh):
    in_specs = (
        P("row", "gx", "gy"),
        P("gx", "gy"),
        P("gx", "gy"),
        P("gx", "gy"),
        P("gx", "gy"),
        P("row", "gy", None),
    )
    out_specs = P("row", "gx", "gy")
    return jax.shard_map(
        on_device, mesh=mesh, in_specs=in_specs, out_specs=out_specs, check_vma=False
    )
```

profile of v0, /device:TPU:28, one launch (start us, length us, event | category | flops | bytes accessed | tf_op | source)
XLA Modules:
  0.0 444.2 jit_solution(13697356211954188351)
XLA Ops:
  10.0 39.7 %all-gather = f32[16,6,64]{2,1,0:T(8,128)S(1)} all-gather(f32[1,6,64]{2,1,0:T(8,128)S(1)} %bitcast.12), channel_id=1, replica_groups=mesh['gx'=8,'gy'=16,'row'=2] {'gy'}, dimensions={0}, use_global_device_ids=true | all-gather | bytes 26112 | tf_op jit(solution)/shard_map/all_gather | solution.py:36
  50.4 36.5 %all_gather.9 = f32[8,96,96]{2,0,1:T(8,128)S(1)} all-gather(f32[8,6,96]{2,0,1:T(8,128)S(1)} %copy-done.2), channel_id=1, replica_groups=mesh['gx'=8,'gy'=16,'row'=2] {'gy'}, dimensions={1}, use_global_device_ids=true | all-gather | bytes 313344 | tf_op jit(solution)/shard_map/all_gather | solution.py:37
  87.7 28.8 %all-gather.1 = f32[8,12,256]{2,1,0:T(8,128)S(1)} all-gather(f32[1,12,256]{2,1,0:T(8,128)S(1)} %bitcast.11), channel_id=1, replica_groups=mesh['gx'=8,'gy'=16,'row'=2] {'gx'}, dimensions={0}, use_global_device_ids=true | all-gather | bytes 110592 | tf_op jit(solution)/shard_map/all_gather | solution.py:44
  116.8 8.5 %collective-permute-start.4 = (f32[8,68,2]{2,1,0:T(8,128)S(1)}, f32[8,68,2]{2,1,0:T(8,128)S(1)}, u32[]{:S(2)}, u32[]{:S(2)}) collective-permute-start(f32[8,68,2]{2,1,0:T(8,128)S(1)} %get-tuple-element.27), channel_id=1, source_target_pairs={{2,0},{4,2},{6,4},{8,6},{10,8},{12,10},{14,12},{16,14},{18,16},{20... | collective-permute-start | bytes 13064 | tf_op jit(solution)/shard_map/ppermute | solution.py:25
  127.2 6.4 %collective-permute-done.4 = f32[8,68,2]{2,1,0:T(8,128)S(1)} collective-permute-done((f32[8,68,2]{2,1,0:T(8,128)S(1)}, f32[8,68,2]{2,1,0:T(8,128)S(1)}, u32[]{:S(2)}, u32[]{:S(2)}) %collective-permute-start.4) | collective-permute-done | bytes 4384 | tf_op jit(solution)/shard_map/ppermute | solution.py:25
  133.7 7.2 %collective-permute-done.5 = f32[8,68,2]{2,1,0:T(8,128)S(1)} collective-permute-done((f32[8,68,2]{2,1,0:T(8,128)S(1)}, f32[8,68,2]{2,1,0:T(8,128)S(1)}, u32[]{:S(2)}, u32[]{:S(2)}) %collective-permute-start.5) | collective-permute-done | bytes 4384 | tf_op jit(solution)/shard_map/ppermute | solution.py:23
  149.9 5.8 %collective-permute-start.7 = (f32[8,64,2]{2,1,0:T(8,128)S(1)}, f32[8,64,2]{2,1,0:T(8,128)S(1)}, u32[]{:S(2)}, u32[]{:S(2)}) collective-permute-start(f32[8,64,2]{2,1,0:T(8,128)S(1)} %get-tuple-element.61), channel_id=1, source_target_pairs={{2,0},{4,2},{6,4},{8,6},{10,8},{12,10},{14,12},{16,14},{18,16},{20... | collective-permute-start | bytes 12296 | tf_op jit(solution)/shard_map/ppermute | solution.py:25
  162.9 6.8 %collective-permute-done.6 = f32[8,64,2]{2,1,0:T(8,128)S(1)} collective-permute-done((f32[8,64,2]{2,1,0:T(8,128)S(1)}, f32[8,64,2]{2,1,0:T(8,128)S(1)}, u32[]{:S(2)}, u32[]{:S(2)}) %collective-permute-start.6) | collective-permute-done | bytes 4128 | tf_op jit(solution)/shard_map/ppermute | solution.py:23
  170.4 6.0 %collective-permute-start.9 = (f32[8,2,256]{2,1,0:T(2,128)S(1)}, f32[8,2,256]{2,1,0:T(2,128)S(1)}, u32[]{:S(2)}, u32[]{:S(2)}) collective-permute-start(f32[8,2,256]{2,1,0:T(2,128)S(1)} %get-tuple-element.57), channel_id=1, source_target_pairs={{0,32},{32,64},{64,96},{96,128},{128,160},{160,192},{192,224},{1,3... | collective-permute-start | bytes 49160 | tf_op jit(solution)/shard_map/ppermute | solution.py:23
  178.3 5.8 %collective-permute-done.8 = f32[8,2,256]{2,1,0:T(2,128)S(1)} collective-permute-done((f32[8,2,256]{2,1,0:T(2,128)S(1)}, f32[8,2,256]{2,1,0:T(2,128)S(1)}, u32[]{:S(2)}, u32[]{:S(2)}) %collective-permute-start.8) | collective-permute-done | bytes 16416 | tf_op jit(solution)/shard_map/ppermute | solution.py:25
  194.6 6.3 %collective-permute-done.13 = f32[8,68,2]{2,1,0:T(8,128)S(1)} collective-permute-done((f32[8,68,2]{2,1,0:T(8,128)S(1)}, f32[8,68,2]{2,1,0:T(8,128)S(1)}, u32[]{:S(2)}, u32[]{:S(2)}) %collective-permute-start.13) | collective-permute-done | bytes 4384 | tf_op jit(solution)/shard_map/ppermute | solution.py:23
  203.5 6.0 %collective-permute-start.10 = (f32[8,2,256]{2,1,0:T(2,128)S(1)}, f32[8,2,256]{2,1,0:T(2,128)S(1)}, u32[]{:S(2)}, u32[]{:S(2)}) collective-permute-start(f32[8,2,256]{2,1,0:T(2,128)S(1)} %get-tuple-element.54), channel_id=1, source_target_pairs={{0,32},{32,64},{64,96},{96,128},{128,160},{160,192},{192,224},{1,3... | collective-permute-start | bytes 49160 | tf_op jit(solution)/shard_map/ppermute | solution.py:23
  225.0 5.8 %collective-permute-start.17 = (f32[8,2,256]{2,1,0:T(2,128)S(1)}, f32[8,2,256]{2,1,0:T(2,128)S(1)}, u32[]{:S(2)}, u32[]{:S(2)}) collective-permute-start(f32[8,2,256]{2,1,0:T(2,128)S(1)} %get-tuple-element.51), channel_id=1, source_target_pairs={{0,32},{32,64},{64,96},{96,128},{128,160},{160,192},{192,224},{1,3... | collective-permute-start | bytes 49160 | tf_op jit(solution)/shard_map/ppermute | solution.py:23
  232.7 11.4 %collective-permute-done.16 = f32[8,2,256]{2,1,0:T(2,128)S(1)} collective-permute-done((f32[8,2,256]{2,1,0:T(2,128)S(1)}, f32[8,2,256]{2,1,0:T(2,128)S(1)}, u32[]{:S(2)}, u32[]{:S(2)}) %collective-permute-start.16) | collective-permute-done | bytes 16416 | tf_op jit(solution)/shard_map/ppermute | solution.py:25
  251.1 5.9 %collective-permute-done.20 = f32[8,68,2]{2,1,0:T(8,128)S(1)} collective-permute-done((f32[8,68,2]{2,1,0:T(8,128)S(1)}, f32[8,68,2]{2,1,0:T(8,128)S(1)}, u32[]{:S(2)}, u32[]{:S(2)}) %collective-permute-start.20) | collective-permute-done | bytes 4384 | tf_op jit(solution)/shard_map/ppermute | solution.py:25
  263.8 6.0 %collective-permute-start.18 = (f32[8,2,256]{2,1,0:T(2,128)S(1)}, f32[8,2,256]{2,1,0:T(2,128)S(1)}, u32[]{:S(2)}, u32[]{:S(2)}) collective-permute-start(f32[8,2,256]{2,1,0:T(2,128)S(1)} %get-tuple-element.48), channel_id=1, source_target_pairs={{0,32},{32,64},{64,96},{96,128},{128,160},{160,192},{192,224},{1,3... | collective-permute-start | bytes 49160 | tf_op jit(solution)/shard_map/ppermute | solution.py:23
  338.2 5.8 %collective-permute-done.32 = f32[8,2,256]{2,1,0:T(2,128)S(1)} collective-permute-done((f32[8,2,256]{2,1,0:T(2,128)S(1)}, f32[8,2,256]{2,1,0:T(2,128)S(1)}, u32[]{:S(2)}, u32[]{:S(2)}) %collective-permute-start.32) | collective-permute-done | bytes 16416 | tf_op jit(solution)/shard_map/ppermute | solution.py:25
  353.8 6.4 %collective-permute-done.37 = f32[8,68,2]{2,1,0:T(8,128)S(1)} collective-permute-done((f32[8,68,2]{2,1,0:T(8,128)S(1)}, f32[8,68,2]{2,1,0:T(8,128)S(1)}, u32[]{:S(2)}, u32[]{:S(2)}) %collective-permute-start.37) | collective-permute-done | bytes 4384 | tf_op jit(solution)/shard_map/ppermute | solution.py:23
  362.9 6.0 %collective-permute-start.34 = (f32[8,2,256]{2,1,0:T(2,128)S(1)}, f32[8,2,256]{2,1,0:T(2,128)S(1)}, u32[]{:S(2)}, u32[]{:S(2)}) collective-permute-start(f32[8,2,256]{2,1,0:T(2,128)S(1)} %get-tuple-element.36), channel_id=1, source_target_pairs={{0,32},{32,64},{64,96},{96,128},{128,160},{160,192},{192,224},{1,3... | collective-permute-start | bytes 49160 | tf_op jit(solution)/shard_map/ppermute | solution.py:23
  378.2 5.8 %collective-permute-done.38 = f32[8,64,2]{2,1,0:T(8,128)S(1)} collective-permute-done((f32[8,64,2]{2,1,0:T(8,128)S(1)}, f32[8,64,2]{2,1,0:T(8,128)S(1)}, u32[]{:S(2)}, u32[]{:S(2)}) %collective-permute-start.38) | collective-permute-done | bytes 4128 | tf_op jit(solution)/shard_map/ppermute | solution.py:23
  384.7 8.8 %collective-permute-start.41 = (f32[8,2,256]{2,1,0:T(2,128)S(1)}, f32[8,2,256]{2,1,0:T(2,128)S(1)}, u32[]{:S(2)}, u32[]{:S(2)}) collective-permute-start(f32[8,2,256]{2,1,0:T(2,128)S(1)} %get-tuple-element.33), channel_id=1, source_target_pairs={{0,32},{32,64},{64,96},{96,128},{128,160},{160,192},{192,224},{1,3... | collective-permute-start | bytes 49160 | tf_op jit(solution)/shard_map/ppermute | solution.py:23
  395.5 8.6 %collective-permute-done.40 = f32[8,2,256]{2,1,0:T(2,128)S(1)} collective-permute-done((f32[8,2,256]{2,1,0:T(2,128)S(1)}, f32[8,2,256]{2,1,0:T(2,128)S(1)}, u32[]{:S(2)}, u32[]{:S(2)}) %collective-permute-start.40) | collective-permute-done | bytes 16416 | tf_op jit(solution)/shard_map/ppermute | solution.py:25
  413.9 6.8 %collective-permute-done.45 = f32[8,68,2]{2,1,0:T(8,128)S(1)} collective-permute-done((f32[8,68,2]{2,1,0:T(8,128)S(1)}, f32[8,68,2]{2,1,0:T(8,128)S(1)}, u32[]{:S(2)}, u32[]{:S(2)}) %collective-permute-start.45) | collective-permute-done | bytes 4384 | tf_op jit(solution)/shard_map/ppermute | solution.py:23
  423.3 6.0 %collective-permute-start.42 = (f32[8,2,256]{2,1,0:T(2,128)S(1)}, f32[8,2,256]{2,1,0:T(2,128)S(1)}, u32[]{:S(2)}, u32[]{:S(2)}) collective-permute-start(f32[8,2,256]{2,1,0:T(2,128)S(1)} %get-tuple-element.30), channel_id=1, source_target_pairs={{0,32},{32,64},{64,96},{96,128},{128,160},{160,192},{192,224},{1,3... | collective-permute-start | bytes 49160 | tf_op jit(solution)/shard_map/ppermute | solution.py:23
  (141 shorter events, 196.1 us)
Async XLA Ops:
  0.9 115.6 %collective-permute-start = (f32[8,2,256]{2,1,0:T(2,128)S(1)}, f32[8,2,256]{2,1,0:T(2,128)S(1)}, u32[]{:S(2)}, u32[]{:S(2)}) collective-permute-start(f32[8,2,256]{2,1,0:T(2,128)S(1)} %get-tuple-element.63), channel_id=1, source_target_pairs={{32,0},{64,32},{96,64},{128,96},{160,128},{192,160},{224,192},{33,... | collective-permute-start | bytes 49160 | tf_op jit(solution)/shard_map/ppermute | solution.py:25
  3.5 113.0 %collective-permute-start.1 = (f32[8,2,256]{2,1,0:T(2,128)S(1)}, f32[8,2,256]{2,1,0:T(2,128)S(1)}, u32[]{:S(2)}, u32[]{:S(2)}) collective-permute-start(f32[8,2,256]{2,1,0:T(2,128)S(1)} %get-tuple-element.64), channel_id=1, source_target_pairs={{0,32},{32,64},{64,96},{96,128},{128,160},{160,192},{192,224},{1,3... | collective-permute-start | bytes 49160 | tf_op jit(solution)/shard_map/ppermute | solution.py:23
  116.8 16.9 %collective-permute-start.4 = (f32[8,68,2]{2,1,0:T(8,128)S(1)}, f32[8,68,2]{2,1,0:T(8,128)S(1)}, u32[]{:S(2)}, u32[]{:S(2)}) collective-permute-start(f32[8,68,2]{2,1,0:T(8,128)S(1)} %get-tuple-element.27), channel_id=1, source_target_pairs={{2,0},{4,2},{6,4},{8,6},{10,8},{12,10},{14,12},{16,14},{18,16},{20... | collective-permute-start | bytes 13064 | tf_op jit(solution)/shard_map/ppermute | solution.py:25
  125.2 15.7 %collective-permute-start.5 = (f32[8,68,2]{2,1,0:T(8,128)S(1)}, f32[8,68,2]{2,1,0:T(8,128)S(1)}, u32[]{:S(2)}, u32[]{:S(2)}) collective-permute-start(f32[8,68,2]{2,1,0:T(8,128)S(1)} %get-tuple-element.28), channel_id=1, source_target_pairs={{0,2},{2,4},{4,6},{6,8},{8,10},{10,12},{12,14},{14,16},{16,18},{18... | collective-permute-start | bytes 13064 | tf_op jit(solution)/shard_map/ppermute | solution.py:23
  141.8 27.9 %collective-permute-start.3 = (f32[8,2,256]{2,1,0:T(2,128)S(1)}, f32[8,2,256]{2,1,0:T(2,128)S(1)}, u32[]{:S(2)}, u32[]{:S(2)}) collective-permute-start(f32[8,2,256]{2,1,0:T(2,128)S(1)} %get-tuple-element.59), channel_id=1, source_target_pairs={{32,0},{64,32},{96,64},{128,96},{160,128},{192,160},{224,192},{33,... | collective-permute-start | bytes 49160 | tf_op jit(solution)/shard_map/ppermute | solution.py:25
  146.1 23.6 %collective-permute-start.2 = (f32[8,2,256]{2,1,0:T(2,128)S(1)}, f32[8,2,256]{2,1,0:T(2,128)S(1)}, u32[]{:S(2)}, u32[]{:S(2)}) collective-permute-start(f32[8,2,256]{2,1,0:T(2,128)S(1)} %get-tuple-element.60), channel_id=1, source_target_pairs={{0,32},{32,64},{64,96},{96,128},{128,160},{160,192},{192,224},{1,3... | collective-permute-start | bytes 49160 | tf_op jit(solution)/shard_map/ppermute | solution.py:23
  149.9 13.0 %collective-permute-start.7 = (f32[8,64,2]{2,1,0:T(8,128)S(1)}, f32[8,64,2]{2,1,0:T(8,128)S(1)}, u32[]{:S(2)}, u32[]{:S(2)}) collective-permute-start(f32[8,64,2]{2,1,0:T(8,128)S(1)} %get-tuple-element.61), channel_id=1, source_target_pairs={{2,0},{4,2},{6,4},{8,6},{10,8},{12,10},{14,12},{16,14},{18,16},{20... | collective-permute-start | bytes 12296 | tf_op jit(solution)/shard_map/ppermute | solution.py:25
  155.7 14.0 %collective-permute-start.6 = (f32[8,64,2]{2,1,0:T(8,128)S(1)}, f32[8,64,2]{2,1,0:T(8,128)S(1)}, u32[]{:S(2)}, u32[]{:S(2)}) collective-permute-start(f32[8,64,2]{2,1,0:T(8,128)S(1)} %get-tuple-element.62), channel_id=1, source_target_pairs={{0,2},{2,4},{4,6},{6,8},{8,10},{10,12},{12,14},{14,16},{16,18},{18... | collective-permute-start | bytes 12296 | tf_op jit(solution)/shard_map/ppermute | solution.py:23
  188.6 12.3 %collective-permute-start.13 = (f32[8,68,2]{2,1,0:T(8,128)S(1)}, f32[8,68,2]{2,1,0:T(8,128)S(1)}, u32[]{:S(2)}, u32[]{:S(2)}) collective-permute-start(f32[8,68,2]{2,1,0:T(8,128)S(1)} %get-tuple-element.26), channel_id=1, source_target_pairs={{0,2},{2,4},{4,6},{6,8},{8,10},{10,12},{12,14},{14,16},{16,18},{18... | collective-permute-start | bytes 13064 | tf_op jit(solution)/shard_map/ppermute | solution.py:23
  201.6 22.8 %collective-permute-start.11 = (f32[8,2,256]{2,1,0:T(2,128)S(1)}, f32[8,2,256]{2,1,0:T(2,128)S(1)}, u32[]{:S(2)}, u32[]{:S(2)}) collective-permute-start(f32[8,2,256]{2,1,0:T(2,128)S(1)} %get-tuple-element.53), channel_id=1, source_target_pairs={{32,0},{64,32},{96,64},{128,96},{160,128},{192,160},{224,192},{33,... | collective-permute-start | bytes 49160 | tf_op jit(solution)/shard_map/ppermute | solution.py:25
  203.5 20.9 %collective-permute-start.10 = (f32[8,2,256]{2,1,0:T(2,128)S(1)}, f32[8,2,256]{2,1,0:T(2,128)S(1)}, u32[]{:S(2)}, u32[]{:S(2)}) collective-permute-start(f32[8,2,256]{2,1,0:T(2,128)S(1)} %get-tuple-element.54), channel_id=1, source_target_pairs={{0,32},{32,64},{64,96},{96,128},{128,160},{160,192},{192,224},{1,3... | collective-permute-start | bytes 49160 | tf_op jit(solution)/shard_map/ppermute | solution.py:23
  230.8 13.4 %collective-permute-start.16 = (f32[8,2,256]{2,1,0:T(2,128)S(1)}, f32[8,2,256]{2,1,0:T(2,128)S(1)}, u32[]{:S(2)}, u32[]{:S(2)}) collective-permute-start(f32[8,2,256]{2,1,0:T(2,128)S(1)} %get-tuple-element.52), channel_id=1, source_target_pairs={{32,0},{64,32},{96,64},{128,96},{160,128},{192,160},{224,192},{33,... | collective-permute-start | bytes 49160 | tf_op jit(solution)/shard_map/ppermute | solution.py:25
  244.4 12.7 %collective-permute-start.20 = (f32[8,68,2]{2,1,0:T(8,128)S(1)}, f32[8,68,2]{2,1,0:T(8,128)S(1)}, u32[]{:S(2)}, u32[]{:S(2)}) collective-permute-start(f32[8,68,2]{2,1,0:T(8,128)S(1)} %get-tuple-element.23), channel_id=1, source_target_pairs={{2,0},{4,2},{6,4},{8,6},{10,8},{12,10},{14,12},{16,14},{18,16},{20... | collective-permute-start | bytes 13064 | tf_op jit(solution)/shard_map/ppermute | solution.py:25
  246.3 14.9 %collective-permute-start.21 = (f32[8,68,2]{2,1,0:T(8,128)S(1)}, f32[8,68,2]{2,1,0:T(8,128)S(1)}, u32[]{:S(2)}, u32[]{:S(2)}) collective-permute-start(f32[8,68,2]{2,1,0:T(8,128)S(1)} %get-tuple-element.24), channel_id=1, source_target_pairs={{0,2},{2,4},{4,6},{6,8},{8,10},{10,12},{12,14},{14,16},{16,18},{18... | collective-permute-start | bytes 13064 | tf_op jit(solution)/shard_map/ppermute | solution.py:23
  261.9 22.4 %collective-permute-start.19 = (f32[8,2,256]{2,1,0:T(2,128)S(1)}, f32[8,2,256]{2,1,0:T(2,128)S(1)}, u32[]{:S(2)}, u32[]{:S(2)}) collective-permute-start(f32[8,2,256]{2,1,0:T(2,128)S(1)} %get-tuple-element.47), channel_id=1, source_target_pairs={{32,0},{64,32},{96,64},{128,96},{160,128},{192,160},{224,192},{33,... | collective-permute-start | bytes 49160 | tf_op jit(solution)/shard_map/ppermute | solution.py:25
  263.8 20.5 %collective-permute-start.18 = (f32[8,2,256]{2,1,0:T(2,128)S(1)}, f32[8,2,256]{2,1,0:T(2,128)S(1)}, u32[]{:S(2)}, u32[]{:S(2)}) collective-permute-start(f32[8,2,256]{2,1,0:T(2,128)S(1)} %get-tuple-element.48), channel_id=1, source_target_pairs={{0,32},{32,64},{64,96},{96,128},{128,160},{160,192},{192,224},{1,3... | collective-permute-start | bytes 49160 | tf_op jit(solution)/shard_map/ppermute | solution.py:23
  271.9 12.4 %collective-permute-start.22 = (f32[8,64,2]{2,1,0:T(8,128)S(1)}, f32[8,64,2]{2,1,0:T(8,128)S(1)}, u32[]{:S(2)}, u32[]{:S(2)}) collective-permute-start(f32[8,64,2]{2,1,0:T(8,128)S(1)} %get-tuple-element.50), channel_id=1, source_target_pairs={{0,2},{2,4},{4,6},{6,8},{8,10},{10,12},{12,14},{14,16},{16,18},{18... | collective-permute-start | bytes 12296 | tf_op jit(solution)/shard_map/ppermute | solution.py:23
  309.1 21.3 %collective-permute-start.27 = (f32[8,2,256]{2,1,0:T(2,128)S(1)}, f32[8,2,256]{2,1,0:T(2,128)S(1)}, u32[]{:S(2)}, u32[]{:S(2)}) collective-permute-start(f32[8,2,256]{2,1,0:T(2,128)S(1)} %get-tuple-element.41), channel_id=1, source_target_pairs={{32,0},{64,32},{96,64},{128,96},{160,128},{192,160},{224,192},{33,... | collective-permute-start | bytes 49160 | tf_op jit(solution)/shard_map/ppermute | solution.py:25
  314.6 15.9 %collective-permute-start.26 = (f32[8,2,256]{2,1,0:T(2,128)S(1)}, f32[8,2,256]{2,1,0:T(2,128)S(1)}, u32[]{:S(2)}, u32[]{:S(2)}) collective-permute-start(f32[8,2,256]{2,1,0:T(2,128)S(1)} %get-tuple-element.42), channel_id=1, source_target_pairs={{0,32},{32,64},{64,96},{96,128},{128,160},{160,192},{192,224},{1,3... | collective-permute-start | bytes 49160 | tf_op jit(solution)/shard_map/ppermute | solution.py:23
  360.9 23.1 %collective-permute-start.35 = (f32[8,2,256]{2,1,0:T(2,128)S(1)}, f32[8,2,256]{2,1,0:T(2,128)S(1)}, u32[]{:S(2)}, u32[]{:S(2)}) collective-permute-start(f32[8,2,256]{2,1,0:T(2,128)S(1)} %get-tuple-element.35), channel_id=1, source_target_pairs={{32,0},{64,32},{96,64},{128,96},{160,128},{192,160},{224,192},{33,... | collective-permute-start | bytes 49160 | tf_op jit(solution)/shard_map/ppermute | solution.py:25
  362.9 21.2 %collective-permute-start.34 = (f32[8,2,256]{2,1,0:T(2,128)S(1)}, f32[8,2,256]{2,1,0:T(2,128)S(1)}, u32[]{:S(2)}, u32[]{:S(2)}) collective-permute-start(f32[8,2,256]{2,1,0:T(2,128)S(1)} %get-tuple-element.36), channel_id=1, source_target_pairs={{0,32},{32,64},{64,96},{96,128},{128,160},{160,192},{192,224},{1,3... | collective-permute-start | bytes 49160 | tf_op jit(solution)/shard_map/ppermute | solution.py:23
  406.3 14.4 %collective-permute-start.45 = (f32[8,68,2]{2,1,0:T(8,128)S(1)}, f32[8,68,2]{2,1,0:T(8,128)S(1)}, u32[]{:S(2)}, u32[]{:S(2)}) collective-permute-start(f32[8,68,2]{2,1,0:T(8,128)S(1)} %get-tuple-element.18), channel_id=1, source_target_pairs={{0,2},{2,4},{4,6},{6,8},{8,10},{10,12},{12,14},{14,16},{16,18},{18... | collective-permute-start | bytes 13064 | tf_op jit(solution)/shard_map/ppermute | solution.py:23
  421.4 21.3 %collective-permute-start.43 = (f32[8,2,256]{2,1,0:T(2,128)S(1)}, f32[8,2,256]{2,1,0:T(2,128)S(1)}, u32[]{:S(2)}, u32[]{:S(2)}) collective-permute-start(f32[8,2,256]{2,1,0:T(2,128)S(1)} %get-tuple-element.29), channel_id=1, source_target_pairs={{32,0},{64,32},{96,64},{128,96},{160,128},{192,160},{224,192},{33,... | collective-permute-start | bytes 49160 | tf_op jit(solution)/shard_map/ppermute | solution.py:25
  423.3 19.4 %collective-permute-start.42 = (f32[8,2,256]{2,1,0:T(2,128)S(1)}, f32[8,2,256]{2,1,0:T(2,128)S(1)}, u32[]{:S(2)}, u32[]{:S(2)}) collective-permute-start(f32[8,2,256]{2,1,0:T(2,128)S(1)} %get-tuple-element.30), channel_id=1, source_target_pairs={{0,32},{32,64},{64,96},{96,128},{128,160},{160,192},{192,224},{1,3... | collective-permute-start | bytes 49160 | tf_op jit(solution)/shard_map/ppermute | solution.py:23
  (30 other events, 288.5 us)
where the time goes:
time: 446 us; the launch traced here: 444 us
  starting transfers between devices  181 us (41%)
  waiting for transfers between devices  143 us (32%)
  blocking collectives  105 us (24%)
  other arithmetic  8.96 us (2%)
  local copies, waits for them, and re-layouts  4.8 us (1%)
    ppermute x24, starting transfers between devices, extended(): lax.ppermute(tail, axis, [(i, (i + 1) % count) for i in range(ends)])  108 us
    ppermute x24, waiting for transfers between devices, extended(): lax.ppermute(head, axis, [((i + 1) % count, i) for i in range(ends)])  78.7 us
    ppermute x24, starting transfers between devices, extended(): lax.ppermute(head, axis, [((i + 1) % count, i) for i in range(ends)])  72.5 us
    ppermute x24, waiting for transfers between devices, extended(): lax.ppermute(tail, axis, [(i, (i + 1) % count) for i in range(ends)])  64 us
    all_gather x1, blocking collectives, on_device(): lax.all_gather(east_modes, 'gy', axis=1, tiled=True)  39.7 us
    all_gather x1, blocking collectives, on_device(): lax.all_gather(mode_coef, 'gy', axis=1, tiled=True)  36.5 us
    all_gather x1, blocking collectives, on_device(): lax.all_gather(north_modes, 'gx', axis=0, tiled=True)  28.8 us
  transfers between devices with their start and end apart: 48, of which 29 were waited for; matrix products, arithmetic and copies ran while one was open for 1% of the time, Pallas kernels for 0%

commit v1 on v0

v1 whole, which is shorter than its diff:
```python
import functools

import jax
import jax.numpy as jnp
from jax import lax
from jax.experimental import pallas as pl
from jax.experimental.pallas import tpu as pltpu
from jax.sharding import PartitionSpec as P

MESH = pl.DeviceIdType.MESH
F32 = jnp.float32
STEPS = 6
HALO = 3 * STEPS
OFF = 24
LANES = 128
SUB = 8
PER = LANES // HALO
UNROLL = 4
SCALE = 0.55 / 24.0
GAIN = 0.03


def roll(x, shift, axis=1):
    shift %= x.shape[axis]
    return pltpu.roll(x, shift, axis) if shift else x


def lane_index():
    return lax.broadcasted_iota(jnp.int32, (SUB, LANES), 1)


def widen(lane, west, t0, t1, east):
    return (
        jnp.where(lane < HALO, west, roll(t0, HALO)),
        jnp.where(lane < 64, roll(t0, 64), roll(t1, 64)),
        jnp.where(lane < LANES - HALO, roll(t1, -HALO), east),
    )


E_LO, E_HI, N_LO, N_HI, V_LO, V_HI, DB_LO, DB_HI, S_LO, S_HI, LL, LH, HL, HH = range(14)


def kernel(
    dims,
    v_hbm,
    bg_hbm,
    d_hbm,
    e_hbm,
    n_hbm,
    c_hbm,
    out_ref,
    v_in,
    db_in,
    e_in,
    n_in,
    c_in,
    pad_c,
    pad_e,
    pad_n,
    cg,
    eg,
    ng,
    e_own,
    e_halo,
    n_edge,
    n_halo,
    vt,
    v_halo,
    db_halo,
    strip,
    strip_halo,
    corner_lo,
    corner_hi,
    panel,
    dens,
    speed,
    vel,
    mod,
    buoy,
    s_e,
    s_n,
    peak,
    flat,
    load_sem,
    send_sem,
    recv_sem,
):
    gx_n, gy_n, y_n, kx, ky = dims
    x_n = gy_n // y_n
    gx, gy = lax.axis_index("gx"), lax.axis_index("gy")
    outer, inner = gy // y_n, lax.rem(gy, y_n)
    lane = lane_index()
    sub = lax.broadcasted_iota(jnp.int32, (SUB, LANES), 0)

    def gxo(o):
        return lax.rem(gx + o + gx_n, gx_n)

    def gyo(o):
        return lax.rem(gy + o + gy_n, gy_n)

    def peer(e, d):
        return lax.rem(outer + e, x_n) * y_n + lax.rem(inner + d, y_n)

    loads = [
        pltpu.make_async_copy(src, dst, load_sem.at[i])
        for i, (src, dst) in enumerate(
            (
                (e_hbm, e_in),
                (n_hbm, n_in),
                (c_hbm, c_in),
                (v_hbm, v_in),
                (d_hbm, db_in.at[0]),
                (bg_hbm, db_in.at[1]),
            )
        )
    ]
    for load in loads:
        load.start()

    partners = [{"gx": gxo(a), "gy": gyo(b)} for a in (-1, 0, 1) for b in (-1, 0, 1) if a or b]
    partners += [{"gy": peer(0, d)} for d in range(1, y_n)]
    partners += [{"gy": peer(e, 0)} for e in range(1, x_n)]
    partners += [{"gx": gxo(o)} for o in range(1, gx_n)]
    barrier = pltpu.get_barrier_semaphore()
    for partner in partners:
        pl.semaphore_signal(barrier, inc=1, device_id=partner, device_id_type=MESH)

    sent = []

    def send(src, dst, slot, target):
        copy = pltpu.make_async_remote_copy(
            src_ref=src,
            dst_ref=dst,
            send_sem=send_sem.at[len(sent)],
            recv_sem=recv_sem.at[slot],
            device_id=target,
            device_id_type=MESH,
        )
        copy.start()
        sent.append(copy)

    def arrived(dst, slot):
        pltpu.make_async_copy(dst, dst, recv_sem.at[slot]).wait()

    c_base = 14
    e_base = c_base + gy_n
    n_base = e_base + gy_n

    pad_c[...] = jnp.zeros_like(pad_c)
    pad_e[...] = jnp.zeros_like(pad_e)
    pad_n[...] = jnp.zeros_like(pad_n)
    for load in loads[:3]:
        load.wait()
    pad_e[0 : e_in.shape[0], 0:ky] = e_in[...]
    pad_n[0:kx, :] = n_in[...]
    pad_c[:, 0:ky, 0 : c_in.shape[2]] = c_in[...]

    e_own[...] = roll(jnp.transpose(pad_e[...])[0:SUB], OFF)
    n0, n1 = (pad_n[0:SUB, 0:LANES], pad_n[0:SUB, LANES:]), (pad_n[SUB:, 0:LANES], pad_n[SUB:, LANES:])
    n_edge[0] = jnp.where(lane < HALO, n0[0], roll(n1[0], HALO))
    n_edge[1] = jnp.where(lane < HALO, roll(n0[1], HALO), roll(n1[1], 2 * HALO))

    spread = []
    for r in range(SUB):
        whole = pad_c[r]
        wide = jnp.zeros_like(whole)
        for block in range(gx_n):
            keep = (lane >= 16 * block) & (lane < 16 * block + kx)
            wide = jnp.where(keep, roll(whole, (16 - kx) * block), wide)
        spread.append(wide)
    for r in range(6):
        extra = spread[6 + r // 3]
        cg[0, r] = jnp.where(sub < ky, spread[r], roll(extra, ky - 2 * (r % 3), 0))

    pl.semaphore_wait(barrier, len(partners))

    send(e_own, e_halo.at[0], E_LO, {"gx": gxo(1)})
    send(e_own, e_halo.at[1], E_HI, {"gx": gxo(-1)})
    send(n_edge.at[1], n_halo.at[0], N_LO, {"gy": gyo(1)})
    send(n_edge.at[0], n_halo.at[1], N_HI, {"gy": gyo(-1)})
    for d in range(1, y_n):
        send(cg.at[0], cg.at[d], c_base + d, {"gy": peer(0, d)})
    for e in range(1, x_n):
        send(cg.at[0], cg.at[e * y_n], c_base + e * y_n, {"gy": peer(e, 0)})

    loads[4].wait()
    loads[5].wait()
    rows = db_in.shape[1]
    send(db_in.at[:, pl.ds(rows - OFF, OFF)], db_halo.at[0], DB_LO, {"gx": gxo(1)})
    send(db_in.at[:, pl.ds(0, OFF)], db_halo.at[1], DB_HI, {"gx": gxo(-1)})

    loads[3].wait()

    @pl.loop(0, rows // SUB)
    def _(a):
        at = pl.multiple_of(a * SUB, SUB)
        for r in range(SUB):
            for t in range(2):
                vt[t, pl.ds(a * SUB * SUB + r, SUB, stride=SUB), :] = v_in[
                    r, pl.ds(at, SUB), t * LANES : (t + 1) * LANES
                ]

    edge = HALO * SUB
    send(vt.at[:, pl.ds(rows * SUB - edge, edge)], v_halo.at[0], V_LO, {"gx": gxo(1)})
    send(vt.at[:, pl.ds(0, edge)], v_halo.at[1], V_HI, {"gx": gxo(-1)})

    def tile(t, i):
        return vt[t, pl.ds(pl.multiple_of(i * SUB, SUB), SUB), :]

    full = rows // PER

    def pack(g, count):
        low = jnp.zeros((SUB, LANES), F32)
        high = jnp.zeros((SUB, LANES), F32)
        for p in range(count):
            here = (lane >= p * HALO) & (lane < (p + 1) * HALO)
            low = jnp.where(here, roll(tile(0, g * PER + p), p * HALO), low)
            high = jnp.where(here, roll(tile(1, g * PER + p), (p + 1) * HALO), high)
        strip[0, 1 + g] = low
        strip[1, 1 + g] = high

    pl.loop(0, full)(lambda g: pack(g, PER))
    slabs = full
    if rows % PER:
        pack(full, rows % PER)
        slabs += 1
    lo_tile, hi_tile = 0, rows // SUB - 3
    groups = ((0, range(0, 3)), (slabs + 1, range(hi_tile, hi_tile + 3)), (slabs + 2, range(3, hi_tile)))
    for slab, blocks in groups:
        low = jnp.zeros((SUB, LANES), F32)
        high = jnp.zeros((SUB, LANES), F32)
        for j, a in enumerate(blocks):
            for q in range(2):
                p = 2 * j + q
                here = (lane >= p * HALO) & (lane < (p + 1) * HALO)
                low = jnp.where(here, roll(db_in[q, a * SUB : (a + 1) * SUB, 0:LANES], p * HALO), low)
                high = jnp.where(here, roll(db_in[q, a * SUB : (a + 1) * SUB, LANES:], (p + 1) * HALO), high)
        strip[0, slab] = low
        strip[1, slab] = high
    first_hi = (rows - HALO) // PER
    lo_len, hi_len = corner_hi.shape[1], corner_lo.shape[1]
    lo_rows, hi_rows = pl.ds(0, lo_len), pl.ds(1 + first_hi, hi_len)
    send(strip.at[1], strip_halo.at[0], S_LO, {"gy": gyo(1)})
    send(strip.at[0], strip_halo.at[1], S_HI, {"gy": gyo(-1)})
    send(strip.at[1, hi_rows], corner_lo.at[0], LL, {"gx": gxo(1), "gy": gyo(1)})
    send(strip.at[0, hi_rows], corner_lo.at[1], LH, {"gx": gxo(1), "gy": gyo(-1)})
    send(strip.at[1, lo_rows], corner_hi.at[0], HL, {"gx": gxo(-1), "gy": gyo(1)})
    send(strip.at[0, lo_rows], corner_hi.at[1], HH, {"gx": gxo(-1), "gy": gyo(-1)})

    arrived(e_halo.at[0], E_LO)
    arrived(e_halo.at[1], E_HI)
    eg[0] = jnp.where(
        lane < OFF, roll(e_halo[0], -rows), jnp.where(lane < OFF + rows, e_own[...], roll(e_halo[1], rows))
    )
    for d in range(1, y_n):
        send(eg.at[0], eg.at[d], e_base + d, {"gy": peer(0, d)})
    for e in range(1, x_n):
        send(eg.at[0], eg.at[e * y_n], e_base + e * y_n, {"gy": peer(e, 0)})
    arrived(n_halo.at[0], N_LO)
    arrived(n_halo.at[1], N_HI)
    for half, (t0, t1) in enumerate((n0, n1)):
        west = roll(n_halo[0], -half * HALO)
        east = roll(n_halo[1], -(half + 1) * HALO)
        for t, value in enumerate(widen(lane, west, t0, t1, east)):
            ng[gx, t, half * SUB : (half + 1) * SUB, :] = value
    for o in range(1, gx_n):
        send(ng.at[gx], ng.at[gx], n_base + o, {"gx": gxo(o)})

    for d in sorted(range(1, y_n), key=lambda d: min(d, y_n - d)):
        arrived(cg.at[d], c_base + d)
        for e in range(1, x_n):
            send(cg.at[d], cg.at[e * y_n + d], c_base + e * y_n + d, {"gy": peer(e, 0)})
    for d in sorted(range(1, y_n), key=lambda d: min(d, y_n - d)):
        arrived(eg.at[d], e_base + d)
        for e in range(1, x_n):
            send(eg.at[d], eg.at[e * y_n + d], e_base + e * y_n + d, {"gy": peer(e, 0)})

    west_in, east_in = gy > 0, gy < gy_n - 1
    low_in, high_in = gx > 0, gx < gx_n - 1
    one = jnp.float32(1.0)
    west_gain, east_gain = jnp.where(west_in, one, 0.0), jnp.where(east_in, one, 0.0)
    low_gain, high_gain = jnp.where(low_in, one, 0.0), jnp.where(high_in, one, 0.0)

    arrived(strip_halo.at[0], S_LO)
    arrived(strip_halo.at[1], S_HI)

    def own_rows(g, count):
        for p in range(count):
            i = g * PER + p
            west = roll(strip_halo[0, 1 + g], -p * HALO) * west_gain
            east = roll(strip_halo[1, 1 + g], -(p + 1) * HALO) * east_gain
            for t, value in enumerate(widen(lane, west, tile(0, i), tile(1, i), east)):
                vel[t, OFF + i] = value

    pl.loop(0, full)(lambda g: own_rows(g, PER))
    if rows % PER:
        own_rows(full, rows % PER)

    for side, slot in ((0, V_LO), (1, V_HI)):
        arrived(v_halo.at[side], slot)
    for side, slot in ((0, LL), (1, LH)):
        arrived(corner_lo.at[side], slot)
    for side, slot in ((0, HL), (1, HH)):
        arrived(corner_hi.at[side], slot)
    zero = jnp.zeros((SUB, LANES), F32)
    for t in range(3):
        for i in range(OFF - HALO):
            vel[t, i] = zero
            vel[t, OFF + rows + HALO + i] = zero
    for i in range(HALO):
        for side, corner, row, at, gain in (
            (0, corner_lo, rows - HALO + i, OFF - HALO + i, low_gain),
            (1, corner_hi, i, OFF + rows + i, high_gain),
        ):
            slab = row // PER - first_hi if side == 0 else 1 + row // PER
            p = row % PER
            west = roll(corner[0, slab], -p * HALO) * west_gain
            east = roll(corner[1, slab], -(p + 1) * HALO) * east_gain
            t0 = v_halo[side, 0, i * SUB : (i + 1) * SUB, :]
            t1 = v_halo[side, 1, i * SUB : (i + 1) * SUB, :]
            for t, value in enumerate(widen(lane, west, t0, t1, east)):
                vel[t, at] = value * gain

    for side, slot in ((0, DB_LO), (1, DB_HI)):
        arrived(db_halo.at[side], slot)
    tiles = rows // SUB
    for b in range(tiles + 6):
        values = []
        for q in range(2):
            if b < 3:
                t0, t1 = (db_halo[0, q, b * SUB : (b + 1) * SUB, t * LANES : (t + 1) * LANES] for t in range(2))
                w, e = (corner_lo[s, hi_len - 1] for s in range(2))
                p = 2 * b + q
            elif b < tiles + 3:
                a = b - 3
                t0, t1 = (db_in[q, a * SUB : (a + 1) * SUB, t * LANES : (t + 1) * LANES] for t in range(2))
                slab, blocks = next(g for g in groups if a in g[1])
                w, e = (strip_halo[s, slab] for s in range(2))
                p = 2 * (a - blocks[0]) + q
            else:
                a = b - 3 - tiles
                t0, t1 = (db_halo[1, q, a * SUB : (a + 1) * SUB, t * LANES : (t + 1) * LANES] for t in range(2))
                w, e = (corner_hi[s, 0] for s in range(2))
                p = 2 * a + q
            values.append(widen(lane, roll(w, -p * HALO), t0, t1, roll(e, -(p + 1) * HALO)))
        for t in range(3):
            d, s = values[0][t], values[1][t]
            gains = ([low_gain] if b < 3 else []) + ([high_gain] if b >= tiles + 3 else [])
            keep = jnp.ones((SUB, LANES), F32)
            if t == 0:
                keep = jnp.where(lane < HALO, west_gain, keep)
            if t == 2:
                keep = jnp.where(lane >= LANES - HALO, east_gain, keep)
            for gain in gains:
                keep = keep * gain
            speed[t, b * SUB : (b + 1) * SUB, :] = (keep * SCALE) * d * s * s
            dens[t, b * SUB : (b + 1) * SUB, :] = (keep * SCALE) / d

    for slot in range(1, gy_n):
        if slot >= y_n:
            arrived(cg.at[slot], c_base + slot)
            arrived(eg.at[slot], e_base + slot)
    depth = gy_n * SUB
    wide_rows = OFF + rows + OFF
    lhs = jnp.transpose(eg[...].reshape(depth, LANES))[0:wide_rows]
    shifted = []
    for s in range(3):
        parts = [jnp.where(sub >= ky, roll(eg[b], ky - 2 * s, 0), 0.0) for b in range(gy_n)]
        shifted.append(jnp.transpose(jnp.concatenate(parts, axis=0))[0:wide_rows])

    def product(a, b):
        return jnp.dot(a, b, precision=lax.Precision.HIGHEST, preferred_element_type=F32)

    last = [None, None]
    for r in range(6):
        rhs = cg[:, r].reshape(depth, LANES)
        panel[pl.ds(r, wide_rows, stride=SUB), :] = product(lhs, rhs)
        term = product(shifted[r % 3], rhs)
        last[r // 3] = term if last[r // 3] is None else last[r // 3] + term
    for r in (6, 7):
        panel[pl.ds(r, wide_rows, stride=SUB), :] = last[r - 6]

    for o in range(1, gx_n):
        at = gxo(-o)
        arrived(ng.at[at], n_base + o)
    if gx_n * 16 < LANES:
        panel_depth = gx_n * 16
    else:
        panel_depth = LANES
    right = jnp.concatenate([ng[:, t].reshape(gx_n * 16, LANES) for t in range(3)], axis=1)

    @pl.loop(0, wide_rows // SUB)
    def _(c):
        at = pl.multiple_of(c * SUB, SUB)
        left = panel[pl.ds(pl.multiple_of(c * SUB * SUB, SUB * SUB), SUB * SUB), :]
        field = product(left[:, 0:panel_depth], right)
        for t in range(3):
            g = speed[t, pl.ds(at, SUB), :]
            w = dens[t, pl.ds(at, SUB), :]
            for u in range(SUB):
                q = 1.0 + GAIN * jnp.tanh(field[u * SUB : (u + 1) * SUB, t * LANES : (t + 1) * LANES])
                mod[t, at + u] = jnp.broadcast_to(g[u : u + 1], (SUB, LANES)) * (q * q)
                buoy[t, at + u] = jnp.broadcast_to(w[u : u + 1], (SUB, LANES))

    for step in range(1, STEPS + 1):
        begin = OFF - HALO + 3 * step - 2
        count = rows + 2 * HALO + 3 - 6 * step
        chunks = -(-count // UNROLL)

        def sweep(c, carry, begin=begin, first=step == 1):
            carry = list(carry)
            for u in range(UNROLL):
                i = begin + c * UNROLL + u
                for t in range(3):
                    vm, v0, v1, e3, e2, e1, n1_ = carry[t]
                    v2 = vel[t, i + 2]
                    m = mod[t, i]
                    ge = 27.0 * (v1 - v0) - (v2 - vm)
                    gn = 27.0 * (roll(v0, -1) - v0) - (roll(v0, -2) - roll(v0, 1))
                    se, sn = m * ge, m * gn
                    if not first:
                        se, sn = s_e[t, i] + se, s_n[t, i] + sn
                    if step < STEPS:
                        s_e[t, i] = se
                        s_n[t, i] = sn
                    near = (e1 - e2) + (n1_ - roll(n1_, 1))
                    far = (se - e3) + (roll(n1_, -1) - roll(n1_, 2))
                    vn = vm + buoy[t, i - 1] * (27.0 * near - far)
                    if step < STEPS:
                        vel[t, i - 1] = vn
                    top = jnp.abs(vn)
                    peak[t, i - 1] = top if first else jnp.maximum(peak[t, i - 1], top)
                    carry[t] = (v0, v1, v2, e2, e1, se, sn)
            return tuple(carry)

        start = tuple(
            (vel[t, begin - 1], vel[t, begin], vel[t, begin + 1], zero, zero, zero, zero) for t in range(3)
        )
        lax.fori_loop(0, chunks, sweep, start)

    cut_a = LANES - 2 * HALO
    cut_b = 174 - LANES

    @pl.loop(0, rows // SUB)
    def _(a):
        for u in range(SUB):
            i = a * SUB + u
            p0, p1, p2 = (peak[t, OFF + i] for t in range(3))
            mid = roll(p1, 64)
            at = pl.multiple_of(i * SUB, SUB)
            flat[0, pl.ds(at, SUB), :] = jnp.where(lane < cut_a, roll(p0, -HALO), mid)
            flat[1, pl.ds(at, SUB), :] = jnp.where(lane < cut_b, mid, roll(p2, HALO))
        at = pl.multiple_of(a * SUB, SUB)
        for r in range(SUB):
            for t in range(2):
                out_ref[r, pl.ds(at, SUB), t * LANES : (t + 1) * LANES] = flat[
                    t, pl.ds(a * SUB * SUB + r, SUB, stride=SUB), :
                ]

    for copy in sent:
        copy.wait_send()


def on_device(gx_n, gy_n, initial_velocity, background_speed, density, east_modes, north_modes, mode_coef):
    reals, rows, cols = initial_velocity.shape
    kx, ky = north_modes.shape[0], east_modes.shape[1]
    y_n = 4 if gy_n == 16 else 2
    x_n = gy_n // y_n
    wide = rows + 2 * OFF
    slabs = -(-rows // PER)
    lo_len = 1 + (HALO - 1) // PER + 1
    hi_len = slabs - (rows - HALO) // PER + 1
    sends = 4 + 2 + 2 + 2 + 4 + 2 * (gy_n - 1) + gx_n - 1
    vmem = lambda *shape: pltpu.VMEM(shape, F32)
    scratch = [
        vmem(reals, rows, cols),
        vmem(2, rows, cols),
        vmem(*east_modes.shape),
        vmem(*north_modes.shape),
        vmem(*mode_coef.shape),
        vmem(reals, SUB, LANES),
        vmem(LANES, LANES),
        vmem(16, cols),
        vmem(gy_n, 6, SUB, LANES),
        vmem(gy_n, SUB, LANES),
        vmem(gx_n, 3, 16, LANES),
        vmem(SUB, LANES),
        vmem(2, SUB, LANES),
        vmem(2, SUB, LANES),
        vmem(2, SUB, LANES),
        vmem(2, rows * SUB, LANES),
        vmem(2, 2, HALO * SUB, LANES),
        vmem(2, 2, OFF, cols),
        vmem(2, slabs + 3, SUB, LANES),
        vmem(2, slabs + 3, SUB, LANES),
        vmem(2, hi_len, SUB, LANES),
        vmem(2, lo_len, SUB, LANES),
        vmem(wide * SUB, LANES),
        vmem(3, wide, LANES),
        vmem(3, wide, LANES),
        vmem(3, wide, SUB, LANES),
        vmem(3, wide, SUB, LANES),
        vmem(3, wide, SUB, LANES),
        vmem(3, wide, SUB, LANES),
        vmem(3, wide, SUB, LANES),
        vmem(3, wide, SUB, LANES),
        vmem(2, rows * SUB, LANES),
        pltpu.SemaphoreType.DMA((6,)),
        pltpu.SemaphoreType.DMA((sends,)),
        pltpu.SemaphoreType.DMA((14 + 2 * gy_n + gx_n,)),
    ]
    return pl.pallas_call(
        functools.partial(kernel, (gx_n, gy_n, y_n, kx, ky)),
        out_shape=jax.ShapeDtypeStruct(initial_velocity.shape, F32),
        in_specs=[pl.BlockSpec(memory_space=pl.ANY)] * 6,
        out_specs=pl.BlockSpec(memory_space=pltpu.VMEM),
        scratch_shapes=scratch,
        compiler_params=pltpu.CompilerParams(
            collective_id=0, has_side_effects=True, vmem_limit_bytes=40 * 1024 * 1024
        ),
    )(initial_velocity, background_speed, density, east_modes, north_modes, mode_coef)


def solution(mesh):
    in_specs = (
        P("row", "gx", "gy"),
        P("gx", "gy"),
        P("gx", "gy"),
        P("gx", "gy"),
        P("gx", "gy"),
        P("row", "gy", None),
    )
    out_specs = P("row", "gx", "gy")
    body = functools.partial(on_device, mesh.shape["gx"], mesh.shape["gy"])
    return jax.shard_map(body, mesh=mesh, in_specs=in_specs, out_specs=out_specs, check_vma=False)
```

time: 446 us -> 62.1 us (0.14)
  the two profiles are of different devices: /device:TPU:28 before, /device:TPU:2 now
where the time goes in v1:
time: 62.1 us; the launch traced here: 61.9 us
  Pallas kernels  57.6 us (93%)
  local copies, waits for them, and re-layouts  4.24 us (7%)
    pallas_call x1, Pallas kernels, on_device(): pl.pallas_call(functools.partial(kernel, (gx_n, gy_n, y_n, kx, ky)), out_...  57.6 us
    unnamed x11, local copies, waits for them, and re-layouts  4.24 us

profile of v1, /device:TPU:2, one launch (start us, length us, event | category | flops | bytes accessed | tf_op | source)
XLA Modules:
  0.0 61.9 jit_solution(5674968884484954406)
XLA Ops:
  0.0 0.0 copy-start.1
  0.0 0.8 %copy.7.e_hbm = f32[64,6]{1,0:T(8,128)S(1)} copy(f32[64,6]{0,1:T(8,128)} %param.9) | data formatting | bytes 3072 | tf_op args[3]
  0.8 0.0 copy-start.3
  0.8 0.8 %copy.8.c_hbm = f32[8,6,96]{2,1,0:T(8,128)S(1)} copy(f32[8,6,96]{2,0,1:T(8,128)} %param.11) | data formatting | bytes 36864 | tf_op args[5]
  1.6 0.0 copy-done.1
  1.6 0.0 copy-done.3
  1.6 0.0 copy-start
  1.6 1.0 %copy-done = f32[8,64,256]{2,1,0:T(8,128)S(1)} copy-done((f32[8,64,256]{2,1,0:T(8,128)S(1)}, f32[8,64,256]{2,1,0:T(8,128)}, u32[]{:S(2)}) %copy-start) | copy-done | bytes 524312
  2.6 0.0 copy-start.2
  2.6 0.8 %copy-done.2 = f32[64,256]{1,0:T(8,128)S(1)} copy-done((f32[64,256]{1,0:T(8,128)S(1)}, f32[64,256]{1,0:T(8,128)}, u32[]{:S(2)}) %copy-start.2) | copy-done | bytes 65560
  3.5 57.6 %shard_map.64 = f32[8,64,256]{2,1,0:T(8,128)S(1)} custom-call(f32[8,64,256]{2,1,0:T(8,128)S(1)} %copy-done, f32[64,256]{1,0:T(8,128)S(1)} %copy-done.1, f32[64,256]{1,0:T(8,128)S(1)} %copy-done.2, f32[64,6]{1,0:T(8,128)S(1)} %copy.7.e_hbm, f32[12,256]{1,0:T(8,128)S(1)} %copy-done.3, f32[8,6,96]{2,1,0:T(8,128)S(1)} %copy.8.c_hbm), custom_call_target="tpu_custom_call" | custom-call | tf_op jit(solution)/shard_map/pallas_call | solution.py:512
  61.1 0.8 %copy.10 = f32[8,64,256]{2,1,0:T(8,128)} copy(f32[8,64,256]{2,1,0:T(8,128)S(1)} %shard_map.64) | data formatting | bytes 1048576
Async XLA Ops:
  0.0 1.6 %copy-start.1 = (f32[64,256]{1,0:T(8,128)S(1)}, f32[64,256]{1,0:T(8,128)}, u32[]{:S(2)}) copy-start(f32[64,256]{1,0:T(8,128)} %bg_hbm.1) | copy-start | bytes 196612
  0.8 0.8 %copy-start.3 = (f32[12,256]{1,0:T(8,128)S(1)}, f32[12,256]{1,0:T(8,128)}, u32[]{:S(2)}) copy-start(f32[12,256]{1,0:T(8,128)} %n_hbm.1) | copy-start | bytes 36868
  1.6 1.0 %copy-start = (f32[8,64,256]{2,1,0:T(8,128)S(1)}, f32[8,64,256]{2,1,0:T(8,128)}, u32[]{:S(2)}) copy-start(f32[8,64,256]{2,1,0:T(8,128)} %v_hbm.1) | copy-start | bytes 1572868
  2.6 0.8 %copy-start.2 = (f32[64,256]{1,0:T(8,128)S(1)}, f32[64,256]{1,0:T(8,128)}, u32[]{:S(2)}) copy-start(f32[64,256]{1,0:T(8,128)} %d_hbm.1) | copy-start | bytes 196612

commit v2 on v1

v2 whole, which is shorter than its diff:
```python
import functools

import jax
import jax.numpy as jnp
from jax import lax
from jax.experimental import pallas as pl
from jax.experimental.pallas import tpu as pltpu
from jax.sharding import PartitionSpec as P

MESH = pl.DeviceIdType.MESH
F32 = jnp.float32
STEPS = 6
HALO = 3 * STEPS
OFF = 24
LANES = 128
SUB = 8
PER = LANES // HALO
PLANES = 5
HALF = LANES // 2
WIDE = PLANES * LANES
UNROLL = 4
BF16 = jnp.bfloat16
SCALE = 0.55 / 24.0
GAIN = 0.03


def roll(x, shift, axis=1):
    shift %= x.shape[axis]
    return pltpu.roll(x, shift, axis) if shift else x


def lane_index():
    return lax.broadcasted_iota(jnp.int32, (SUB, LANES), 1)


def pieces(x):
    high = x.astype(BF16)
    rest = x - high.astype(F32)
    mid = rest.astype(BF16)
    low = (rest - mid.astype(F32)).astype(BF16)
    return jnp.concatenate([high, mid, low], axis=0)


def fold(x):
    n = x.shape[0] // 3
    return x[0:n] + (x[n : 2 * n] + x[2 * n :])


def moved(x, deal):
    return fold(jnp.dot(pieces(x), deal, preferred_element_type=F32))


E_LO, E_HI, N_LO, N_HI, V_LO, V_HI, DB_LO, DB_HI, S_LO, S_HI, LL, LH, HL, HH = range(14)


def kernel(
    dims,
    v_hbm,
    bg_hbm,
    d_hbm,
    e_hbm,
    n_hbm,
    c_hbm,
    out_ref,
    v_in,
    db_in,
    e_in,
    n_in,
    pad_e,
    pad_n,
    c_got,
    c_all,
    eg,
    e_all,
    ng,
    n_all,
    n_parts,
    e_halo,
    n_edge,
    n_halo,
    nat,
    side,
    db_halo,
    strip,
    strip_halo,
    corner_lo,
    corner_hi,
    deal_own,
    deal_side,
    panel,
    g_nat,
    b_nat,
    g_wide,
    b_wide,
    vel,
    mod,
    buoy,
    s_e,
    s_n,
    peak,
    flat,
    load_sem,
    send_sem,
    recv_sem,
):
    gx_n, gy_n, y_n, kx, ky = dims
    x_n = gy_n // y_n
    gx, gy = lax.axis_index("gx"), lax.axis_index("gy")
    outer, inner = gy // y_n, lax.rem(gy, y_n)
    lane = lane_index()
    rows = v_hbm.shape[1]
    half_rows = rows // 2
    modes = gy_n * ky

    def gxo(o):
        return lax.rem(gx + o + gx_n, gx_n)

    def gyo(o):
        return lax.rem(gy + o + gy_n, gy_n)

    def peer(e, d):
        return lax.rem(outer + e, x_n) * y_n + lax.rem(inner + d, y_n)

    mid_rows = rows - 2 * OFF
    bands = ((0, OFF), (rows - OFF, OFF), (OFF, mid_rows))
    moves = [(n_hbm, n_in), (d_hbm, db_in.at[0]), (bg_hbm, db_in.at[1])]
    moves += [(v_hbm.at[:, pl.ds(a, n)], v_in.at[:, pl.ds(a, n)]) for a, n in bands]
    moves += [(e_hbm, e_in), (c_hbm, c_got.at[0])]
    loads = [pltpu.make_async_copy(src, dst, load_sem.at[i]) for i, (src, dst) in enumerate(moves)]
    for load in loads:
        load.start()

    partners = [{"gx": gxo(a), "gy": gyo(b)} for a in (-1, 0, 1) for b in (-1, 0, 1) if a or b]
    partners += [{"gy": peer(0, d)} for d in range(1, y_n)]
    partners += [{"gy": peer(e, 0)} for e in range(1, x_n)]
    partners += [{"gx": gxo(o)} for o in range(1, gx_n)]
    barrier = pltpu.get_barrier_semaphore()
    for partner in partners:
        pl.semaphore_signal(barrier, inc=1, device_id=partner, device_id_type=MESH)

    sent = []

    def send(src, dst, slot, target):
        copy = pltpu.make_async_remote_copy(
            src_ref=src,
            dst_ref=dst,
            send_sem=send_sem.at[len(sent)],
            recv_sem=recv_sem.at[slot],
            device_id=target,
            device_id_type=MESH,
        )
        copy.start()
        sent.append(copy)

    def arrived(dst, slot):
        pltpu.make_async_copy(dst, dst, recv_sem.at[slot]).wait()

    c_base = 14
    e_base = c_base + gy_n
    n_base = e_base + gy_n

    pad_e[...] = jnp.zeros_like(pad_e)
    pad_n[...] = jnp.zeros_like(pad_n)
    e_all[...] = jnp.zeros_like(e_all)
    n_all[...] = jnp.zeros_like(n_all)

    pl.semaphore_wait(barrier, len(partners))

    send(e_hbm, e_halo.at[0], E_LO, {"gx": gxo(1)})
    send(e_hbm, e_halo.at[1], E_HI, {"gx": gxo(-1)})
    for d in range(1, y_n):
        send(c_hbm, c_got.at[d], c_base + d, {"gy": peer(0, d)})
    for e in range(1, x_n):
        send(c_hbm, c_got.at[e * y_n], c_base + e * y_n, {"gy": peer(e, 0)})

    loads[0].wait()
    pad_n[0:kx, :] = n_in[...]
    n0, n1 = (pad_n[0:SUB, 0:LANES], pad_n[0:SUB, LANES:]), (pad_n[SUB:, 0:LANES], pad_n[SUB:, LANES:])
    n_edge[0] = jnp.where(lane < HALO, n0[0], roll(n1[0], HALO))
    n_edge[1] = jnp.where(lane < HALO, roll(n0[1], HALO), roll(n1[1], 2 * HALO))
    send(n_edge.at[1], n_halo.at[0], N_LO, {"gy": gyo(1)})
    send(n_edge.at[0], n_halo.at[1], N_HI, {"gy": gyo(-1)})

    loads[1].wait()
    loads[2].wait()
    send(db_in.at[:, pl.ds(rows - OFF, OFF)], db_halo.at[0], DB_LO, {"gx": gxo(1)})
    send(db_in.at[:, pl.ds(0, OFF)], db_halo.at[1], DB_HI, {"gx": gxo(-1)})

    def lead(a):
        at = pl.multiple_of(a * SUB, SUB)
        for r in range(SUB):
            for t in range(2):
                nat[t, pl.ds((OFF + a * SUB) * SUB + r, SUB, stride=SUB), :] = v_in[
                    r, pl.ds(at, SUB), t * LANES : (t + 1) * LANES
                ]

    edge = HALO * SUB

    def own(first):
        return nat.at[:, pl.ds((OFF + first) * SUB, edge)]

    for k, (first, count) in enumerate(bands):
        loads[3 + k].wait()
        pl.loop(first // SUB, (first + count) // SUB)(lead)
        if k == 0:
            send(own(0), own(rows), V_HI, {"gx": gxo(-1)})
        if k == 1:
            send(own(rows - HALO), own(-HALO), V_LO, {"gx": gxo(1)})

    def tile(t, i):
        return nat[t, pl.ds(pl.multiple_of((OFF + i) * SUB, SUB), SUB), :]

    full = rows // PER

    def pack(g, count):
        low = jnp.zeros((SUB, LANES), F32)
        high = jnp.zeros((SUB, LANES), F32)
        for p in range(count):
            here = (lane >= p * HALO) & (lane < (p + 1) * HALO)
            low = jnp.where(here, roll(tile(0, g * PER + p), p * HALO), low)
            high = jnp.where(here, roll(tile(1, g * PER + p), (p + 1) * HALO), high)
        strip[0, 1 + g] = low
        strip[1, 1 + g] = high

    pl.loop(0, full)(lambda g: pack(g, PER))
    slabs = full
    if rows % PER:
        pack(full, rows % PER)
        slabs += 1
    hi_tile = rows // SUB - 3
    groups = ((0, range(0, 3)), (slabs + 1, range(hi_tile, hi_tile + 3)), (slabs + 2, range(3, hi_tile)))
    for slab, blocks in groups:
        low = jnp.zeros((SUB, LANES), F32)
        high = jnp.zeros((SUB, LANES), F32)
        for j, a in enumerate(blocks):
            for q in range(2):
                p = 2 * j + q
                here = (lane >= p * HALO) & (lane < (p + 1) * HALO)
                low = jnp.where(here, roll(db_in[q, a * SUB : (a + 1) * SUB, 0:LANES], p * HALO), low)
                high = jnp.where(here, roll(db_in[q, a * SUB : (a + 1) * SUB, LANES:], (p + 1) * HALO), high)
        strip[0, slab] = low
        strip[1, slab] = high
    first_hi = (rows - HALO) // PER
    lo_len, hi_len = corner_hi.shape[1], corner_lo.shape[1]
    lo_rows, hi_rows = pl.ds(0, lo_len), pl.ds(1 + first_hi, hi_len)
    send(strip.at[1], strip_halo.at[0], S_LO, {"gy": gyo(1)})
    send(strip.at[0], strip_halo.at[1], S_HI, {"gy": gyo(-1)})
    send(strip.at[1, hi_rows], corner_lo.at[0], LL, {"gx": gxo(1), "gy": gyo(1)})
    send(strip.at[0, hi_rows], corner_lo.at[1], LH, {"gx": gxo(1), "gy": gyo(-1)})
    send(strip.at[1, lo_rows], corner_hi.at[0], HL, {"gx": gxo(-1), "gy": gyo(1)})
    send(strip.at[0, lo_rows], corner_hi.at[1], HH, {"gx": gxo(-1), "gy": gyo(-1)})

    for half in range(2):
        for p in range(PLANES):
            for ref, n in ((deal_own, 2 * LANES), (deal_side, LANES)):
                k = lax.broadcasted_iota(jnp.int32, (n, LANES), 0)
                l = lax.broadcasted_iota(jnp.int32, (n, LANES), 1) - half * HALF
                if n == LANES:
                    index = jnp.where(k < HALO, k, jnp.where(k < 2 * HALO, k + 2 * LANES, -1))
                else:
                    index = k + HALO
                hit = (PLANES * l + p == index) & (l >= 0) & (l < HALF)
                ref[half * n : (half + 1) * n, p * LANES : (p + 1) * LANES] = jnp.where(hit, 1.0, 0.0).astype(BF16)

    loads[6].wait()
    arrived(e_halo.at[0], E_LO)
    arrived(e_halo.at[1], E_HI)
    for k, piece in enumerate((e_halo[0], e_in[...], e_halo[1])):
        pad_e[k, 0:ky, 0:rows] = piece
    eg[0] = jnp.where(
        lane < OFF,
        roll(pad_e[0], OFF - rows),
        jnp.where(lane < OFF + rows, roll(pad_e[1], OFF), roll(pad_e[2], OFF + rows)),
    )
    for d in range(1, y_n):
        send(eg.at[0], eg.at[d], e_base + d, {"gy": peer(0, d)})
    for e in range(1, x_n):
        send(eg.at[0], eg.at[e * y_n], e_base + e * y_n, {"gy": peer(e, 0)})
    arrived(n_halo.at[0], N_LO)
    arrived(n_halo.at[1], N_HI)

    def flank(west, east):
        return jnp.where(lane < HALO, west, jnp.where(lane < 2 * HALO, east, 0.0))

    for half, (t0, t1) in enumerate((n0, n1)):
        beside = flank(roll(n_halo[0], -half * HALO), roll(n_halo[1], (1 - half) * HALO))
        for t, value in enumerate((t0, t1, beside)):
            ng[gx, t, half * SUB : (half + 1) * SUB, :] = value
    for o in range(1, gx_n):
        send(ng.at[gx], ng.at[gx], n_base + o, {"gx": gxo(o)})

    for d in sorted(range(1, y_n), key=lambda d: min(d, y_n - d)):
        arrived(c_got.at[d], c_base + d)
        for e in range(1, x_n):
            send(c_got.at[d], c_got.at[e * y_n + d], c_base + e * y_n + d, {"gy": peer(e, 0)})
        arrived(eg.at[d], e_base + d)
        for e in range(1, x_n):
            send(eg.at[d], eg.at[e * y_n + d], e_base + e * y_n + d, {"gy": peer(e, 0)})

    one = jnp.float32(1.0)
    west_gain, east_gain = jnp.where(gy > 0, one, 0.0), jnp.where(gy < gy_n - 1, one, 0.0)
    low_gain, high_gain = jnp.where(gx > 0, one, 0.0), jnp.where(gx < gx_n - 1, one, 0.0)

    arrived(strip_halo.at[0], S_LO)
    arrived(strip_halo.at[1], S_HI)

    def unpack(west, east, p):
        return flank(roll(west, -p * HALO) * west_gain, roll(east, (1 - p) * HALO) * east_gain)

    def own_sides(g, count):
        for p in range(count):
            at = pl.multiple_of((OFF + g * PER + p) * SUB, SUB)
            side[pl.ds(at, SUB), :] = unpack(strip_halo[0, 1 + g], strip_halo[1, 1 + g], p)

    pl.loop(0, full)(lambda g: own_sides(g, PER))
    if rows % PER:
        own_sides(full, rows % PER)

    arrived(own(-HALO), V_LO)
    arrived(own(rows), V_HI)
    for s, slot in ((0, LL), (1, LH)):
        arrived(corner_lo.at[s], slot)
    for s, slot in ((0, HL), (1, HH)):
        arrived(corner_hi.at[s], slot)
    for i in range(HALO):
        for corner, row, at, slab, gain in (
            (corner_lo, rows - HALO + i, OFF - HALO + i, (rows - HALO + i) // PER - first_hi, low_gain),
            (corner_hi, i, OFF + rows + i, 1 + i // PER, high_gain),
        ):
            here = slice(at * SUB, (at + 1) * SUB)
            side[here, :] = unpack(corner[0, slab], corner[1, slab], row % PER) * gain
            for t in range(2):
                nat[t, here, :] = nat[t, here, :] * gain

    def dealt(natural, first, count, apart):
        near, far = pl.ds(first, count), pl.ds(first + apart, count)
        wide = jnp.concatenate([natural(t, at) for at in (near, far) for t in range(2)], axis=1)
        sides = jnp.concatenate([natural(2, at) for at in (near, far)], axis=1)
        return fold(
            jnp.dot(pieces(wide), deal_own[...], preferred_element_type=F32)
            + jnp.dot(pieces(sides), deal_side[...], preferred_element_type=F32)
        )

    wide_rows = vel.shape[1]
    chunk = 16

    @pl.loop(0, wide_rows // chunk)
    def _(c):
        first = pl.multiple_of(c * chunk * SUB, chunk * SUB)
        out = dealt(lambda t, at: nat[t, at, :] if t < 2 else side[at, :], first, chunk * SUB, half_rows * SUB)
        for u in range(chunk):
            for p in range(PLANES):
                vel[p, c * chunk + u] = out[u * SUB : (u + 1) * SUB, p * LANES : (p + 1) * LANES]

    for s, slot in ((0, DB_LO), (1, DB_HI)):
        arrived(db_halo.at[s], slot)
    tiles = rows // SUB
    for b in range(tiles + 6):
        values = []
        for q in range(2):
            if b < 3:
                body, a = db_halo.at[0, q], b
                w, e = (corner_lo[s, hi_len - 1] for s in range(2))
                p = 2 * b + q
            elif b < tiles + 3:
                body, a = db_in.at[q], b - 3
                slab, blocks = next(g for g in groups if a in g[1])
                w, e = (strip_halo[s, slab] for s in range(2))
                p = 2 * (a - blocks[0]) + q
            else:
                body, a = db_halo.at[1, q], b - 3 - tiles
                w, e = (corner_hi[s, 0] for s in range(2))
                p = 2 * a + q
            t0, t1 = (body[a * SUB : (a + 1) * SUB, t * LANES : (t + 1) * LANES] for t in range(2))
            values.append((t0, t1, flank(roll(w, -p * HALO), roll(e, (1 - p) * HALO))))
        gain = low_gain if b < 3 else high_gain if b >= tiles + 3 else one
        here = slice(b * SUB, (b + 1) * SUB)
        for t in range(3):
            d, s = values[0][t], values[1][t]
            keep = SCALE * gain
            if t == 2:
                keep = jnp.where(lane < HALO, west_gain, east_gain) * keep
                d = jnp.where(lane < 2 * HALO, d, 1.0)
            g_nat[t, here, :] = keep * d * s * s
            b_nat[t, here, :] = keep / d
    for natural, out in ((g_nat, g_wide), (b_nat, b_wide)):
        out[...] = dealt(lambda t, at, natural=natural: natural[t, at, :], 0, wide_rows, half_rows)

    for slot in range(y_n, gy_n):
        arrived(c_got.at[slot], c_base + slot)
        arrived(eg.at[slot], e_base + slot)
    loads[7].wait()
    c_all[...] = jnp.zeros_like(c_all)
    for slot in range(gy_n):
        e_all[slot * ky : (slot + 1) * ky, :] = eg[slot, 0:ky, :]
        for k in range(ky):
            at = (slot * ky + k) * SUB
            c_all[at : at + SUB, 0 : c_got.shape[3]] = c_got[slot, k]
    nat_rows = OFF + rows + OFF
    lhs = jnp.transpose(e_all[...])[0:nat_rows, 0:modes]
    for r in range(SUB):
        rhs = c_all[pl.ds(r, modes, stride=SUB), :]
        panel[pl.ds(r, nat_rows, stride=SUB), :] = jnp.dot(
            lhs, rhs, precision=lax.Precision.HIGHEST, preferred_element_type=F32
        )

    for o in range(1, gx_n):
        at = gxo(-o)
        arrived(ng.at[at], n_base + o)
    for b in range(gx_n):
        for t in range(3):
            n_all[b * kx : (b + 1) * kx, t * LANES : (t + 1) * LANES] = ng[b, t, 0:kx, :]
    split = pieces(n_all[...])
    lower = jnp.dot(split[:, 0 : 2 * LANES], deal_own[0 : 2 * LANES, :], preferred_element_type=F32)
    lower += jnp.dot(split[:, 2 * LANES :], deal_side[0:LANES, :], preferred_element_type=F32)
    for p in range(PLANES):
        at = slice(p * LANES, (p + 1) * LANES)
        for j in range(3):
            part = lower[j * LANES : (j + 1) * LANES, at]
            n_parts[j, 0:LANES, at] = part.astype(BF16)
            n_parts[j, LANES:, at] = roll(part, HALF).astype(BF16)

    @pl.loop(0, wide_rows // chunk)
    def _(c):
        n = chunk * SUB
        near = pl.ds(pl.multiple_of(c * n, n), n)
        far = pl.ds(pl.multiple_of(c * n + half_rows * SUB, SUB), n)
        left = pieces(jnp.concatenate([panel[near, :], panel[far, :]], axis=1))
        a = jnp.dot(left, n_parts[0], preferred_element_type=F32)
        b = jnp.dot(left[0 : 2 * n], n_parts[1], preferred_element_type=F32)
        field = a[0:n] + (
            (a[n : 2 * n] + b[0:n])
            + (a[2 * n :] + b[n:] + jnp.dot(left[0:n], n_parts[2], preferred_element_type=F32))
        )
        for p in range(PLANES):
            at = slice(p * LANES, (p + 1) * LANES)
            first = pl.multiple_of(c * chunk, chunk)
            g, w = g_wide[pl.ds(first, chunk), at], b_wide[pl.ds(first, chunk), at]
            for u in range(chunk):
                q = 1.0 + GAIN * jnp.tanh(field[u * SUB : (u + 1) * SUB, at])
                mod[p, c * chunk + u] = jnp.broadcast_to(g[u : u + 1], (SUB, LANES)) * (q * q)
                buoy[p, c * chunk + u] = jnp.broadcast_to(w[u : u + 1], (SUB, LANES))

    zero = jnp.zeros((SUB, LANES), F32)
    for step in range(1, STEPS + 1):
        begin = OFF - HALO + 3 * step - 2
        count = half_rows + 2 * HALO + 3 - 6 * step
        chunks = -(-count // UNROLL)

        def sweep(c, carry, begin=begin, first=step == 1):
            carry = list(carry)
            for u in range(UNROLL):
                i = begin + c * UNROLL + u
                v0 = [carry[p][1] for p in range(PLANES)]
                n1_ = [carry[p][6] for p in range(PLANES)]
                v0 += [roll(v0[0], -1), roll(v0[1], -1), roll(v0[-1], 1)]
                n1_ += [roll(n1_[0], -1), roll(n1_[-2], 1), roll(n1_[-1], 1)]
                for p in range(PLANES):
                    vm, _, v1, e3, e2, e1, _ = carry[p]
                    v2 = vel[p, i + 2]
                    m = mod[p, i]
                    ge = 27.0 * (v1 - v0[p]) - (v2 - vm)
                    gn = 27.0 * (v0[p + 1] - v0[p]) - (v0[p + 2] - v0[p - 1])
                    se, sn = m * ge, m * gn
                    if not first:
                        se, sn = s_e[p, i] + se, s_n[p, i] + sn
                    if step < STEPS:
                        s_e[p, i] = se
                        s_n[p, i] = sn
                    near = (e1 - e2) + (n1_[p] - n1_[p - 1])
                    far = (se - e3) + (n1_[p + 1] - n1_[p - 2])
                    vn = vm + buoy[p, i - 1] * (27.0 * near - far)
                    if step < STEPS:
                        vel[p, i - 1] = vn
                    top = jnp.abs(vn)
                    peak[p, i - 1] = top if first else jnp.maximum(peak[p, i - 1], top)
                    carry[p] = (v0[p], v1, v2, e2, e1, se, sn)
            return tuple(carry)

        start = tuple(
            (vel[p, begin - 1], vel[p, begin], vel[p, begin + 1], zero, zero, zero, zero) for p in range(PLANES)
        )
        lax.fori_loop(0, chunks, sweep, start)

    @pl.loop(0, half_rows // SUB)
    def _(a):
        at = pl.multiple_of(a * SUB, SUB)
        block = jnp.concatenate(
            [
                jnp.concatenate([peak[p, OFF + a * SUB + u] for u in range(SUB)], axis=0)
                for p in range(PLANES)
            ],
            axis=1,
        )
        back = fold(
            lax.dot_general(
                pieces(block), deal_own[...], (((1,), (1,)), ((), ())), preferred_element_type=F32
            )
        )
        for t in range(4):
            flat[t] = back[:, t * LANES : (t + 1) * LANES]
            upper = pl.multiple_of(at + (t // 2) * half_rows, SUB)
            for r in range(SUB):
                out_ref[r, pl.ds(upper, SUB), (t % 2) * LANES : (t % 2 + 1) * LANES] = flat[
                    t, pl.ds(r, SUB, stride=SUB), :
                ]

    for copy in sent:
        copy.wait_send()


def on_device(gx_n, gy_n, initial_velocity, background_speed, density, east_modes, north_modes, mode_coef):
    reals, rows, cols = initial_velocity.shape
    kx, ky = north_modes.shape[0], east_modes.shape[1]
    y_n = 4 if gy_n == 16 else 2
    x_n = gy_n // y_n
    wide = rows // 2 + 2 * OFF
    natural = rows + 2 * OFF
    slabs = -(-rows // PER)
    lo_len = 1 + (HALO - 1) // PER + 1
    hi_len = slabs - (rows - HALO) // PER + 1
    sends = 4 + 2 + 2 + 2 + 4 + 2 * (gy_n - 1) + gx_n - 1
    vmem = lambda *shape: pltpu.VMEM(shape, F32)
    scratch = [
        vmem(reals, rows, cols),
        vmem(2, rows, cols),
        vmem(ky, rows),
        vmem(kx, cols),
        vmem(3, SUB, LANES),
        vmem(16, cols),
        vmem(gy_n, ky, reals, mode_coef.shape[2]),
        vmem(gy_n * ky * reals, LANES),
        vmem(gy_n, SUB, LANES),
        vmem(LANES, LANES),
        vmem(gx_n, 3, 16, LANES),
        vmem(LANES, 3 * LANES),
        pltpu.VMEM((3, 2 * LANES, WIDE), BF16),
        vmem(2, ky, rows),
        vmem(2, SUB, LANES),
        vmem(2, SUB, LANES),
        vmem(2, natural * SUB, LANES),
        vmem(natural * SUB, LANES),
        vmem(2, 2, OFF, cols),
        vmem(2, slabs + 3, SUB, LANES),
        vmem(2, slabs + 3, SUB, LANES),
        vmem(2, hi_len, SUB, LANES),
        vmem(2, lo_len, SUB, LANES),
        pltpu.VMEM((4 * LANES, WIDE), BF16),
        pltpu.VMEM((2 * LANES, WIDE), BF16),
        vmem(natural * SUB, LANES),
        vmem(3, natural, LANES),
        vmem(3, natural, LANES),
        vmem(wide, WIDE),
        vmem(wide, WIDE),
        vmem(PLANES, wide, SUB, LANES),
        vmem(PLANES, wide, SUB, LANES),
        vmem(PLANES, wide, SUB, LANES),
        vmem(PLANES, wide, SUB, LANES),
        vmem(PLANES, wide, SUB, LANES),
        vmem(PLANES, wide, SUB, LANES),
        vmem(4, SUB * SUB, LANES),
        pltpu.SemaphoreType.DMA((8,)),
        pltpu.SemaphoreType.DMA((sends,)),
        pltpu.SemaphoreType.DMA((14 + 2 * gy_n + gx_n,)),
    ]
    return pl.pallas_call(
        functools.partial(kernel, (gx_n, gy_n, y_n, kx, ky)),
        out_shape=jax.ShapeDtypeStruct(initial_velocity.shape, F32),
        in_specs=[pl.BlockSpec(memory_space=pl.ANY)] * 6,
        out_specs=pl.BlockSpec(memory_space=pltpu.VMEM),
        scratch_shapes=scratch,
        compiler_params=pltpu.CompilerParams(
            collective_id=0, has_side_effects=True, vmem_limit_bytes=60 * 1024 * 1024
        ),
    )(
        initial_velocity,
        background_speed,
        density,
        jnp.transpose(east_modes),
        north_modes,
        jnp.transpose(mode_coef, (1, 0, 2)),
    )


def solution(mesh):
    in_specs = (
        P("row", "gx", "gy"),
        P("gx", "gy"),
        P("gx", "gy"),
        P("gx", "gy"),
        P("gx", "gy"),
        P("row", "gy", None),
    )
    out_specs = P("row", "gx", "gy")
    body = functools.partial(on_device, mesh.shape["gx"], mesh.shape["gy"])
    return jax.shard_map(body, mesh=mesh, in_specs=in_specs, out_specs=out_specs, check_vma=False)
```

time: 62.1 us -> 50.1 us (0.81)
  Pallas kernels: 57.6 us -> 48.1 us
  local copies, waits for them, and re-layouts: 4.24 us -> 1.87 us
    pallas_call x1, Pallas kernels: 57.6 us -> 48.1 us  [on_device(): pl.pallas_call(functools.partial(kernel, (gx_n, gy_n, y_n, kx, ky)), out_...]
    unnamed x11 -> x1, local copies, waits for them, and re-layouts: 4.24 us -> 1.87 us
where the time goes in v2:
time: 50.1 us; the launch traced here: 50 us
  Pallas kernels  48.1 us (96%)
  local copies, waits for them, and re-layouts  1.87 us (4%)
    pallas_call x1, Pallas kernels, on_device(): pl.pallas_call(functools.partial(kernel, (gx_n, gy_n, y_n, kx, ky)), out_...  48.1 us
    unnamed x1, local copies, waits for them, and re-layouts  1.87 us

profile of v2, /device:TPU:2, one launch (start us, length us, event | category | flops | bytes accessed | tf_op | source)
XLA Modules:
  0.0 50.0 jit_solution(381243949931397332)
XLA Ops:
  0.0 48.1 %shard_map.64 = f32[8,64,256]{2,1,0:T(8,128)} custom-call(f32[8,64,256]{2,1,0:T(8,128)} %v_hbm.1, f32[64,256]{1,0:T(8,128)} %bg_hbm.1, f32[64,256]{1,0:T(8,128)} %d_hbm.1, f32[6,64]{1,0:T(8,128)} %bitcast.3, f32[12,256]{1,0:T(8,128)} %n_hbm.1, f32[6,8,96]{2,1,0:T(8,128)} %bitcast.2), custom_call_target="tpu_custom_call" | custom-call | tf_op jit(solution)/shard_map/pallas_call | solution.py:566
  48.1 1.9 %copy.8 = f32[8,64,256]{2,1,0:T(8,128)} copy(f32[8,64,256]{2,1,0:T(8,128)} %shard_map.64) | data formatting | bytes 1048576

commit v3 on v2

--- a/solution.py
+++ b/solution.py
@@ -18,7 +18,6 @@
 PLANES = 5
 HALF = LANES // 2
 WIDE = PLANES * LANES
-UNROLL = 4
 BF16 = jnp.bfloat16
 SCALE = 0.55 / 24.0
 GAIN = 0.03
@@ -33,24 +32,20 @@
     return lax.broadcasted_iota(jnp.int32, (SUB, LANES), 1)
 
 
-def pieces(x):
-    high = x.astype(BF16)
-    rest = x - high.astype(F32)
-    mid = rest.astype(BF16)
-    low = (rest - mid.astype(F32)).astype(BF16)
-    return jnp.concatenate([high, mid, low], axis=0)
+def pieces(x, count):
+    parts = []
+    for _ in range(count):
+        parts.append(x.astype(BF16))
+        x = x - parts[-1].astype(F32)
+    return jnp.concatenate(parts, axis=0)
 
 
 def fold(x):
-    n = x.shape[0] // 3
-    return x[0:n] + (x[n : 2 * n] + x[2 * n :])
-
-
-def moved(x, deal):
-    return fold(jnp.dot(pieces(x), deal, preferred_element_type=F32))
-
-
-E_LO, E_HI, N_LO, N_HI, V_LO, V_HI, DB_LO, DB_HI, S_LO, S_HI, LL, LH, HL, HH = range(14)
+    n = x.shape[0] // 2
+    return x[0:n] + x[n:]
+
+
+E_LO, E_HI, N_LO, N_HI, V_LO, V_HI, D_LO, D_HI, B_LO, B_HI, S_LO, S_HI, LL, LH, HL, HH = range(16)
 
 
 def kernel(
@@ -155,7 +150,7 @@
     def arrived(dst, slot):
         pltpu.make_async_copy(dst, dst, recv_sem.at[slot]).wait()
 
-    c_base = 14
+    c_base = 16
     e_base = c_base + gy_n
     n_base = e_base + gy_n
 
@@ -172,6 +167,10 @@
         send(c_hbm, c_got.at[d], c_base + d, {"gy": peer(0, d)})
     for e in range(1, x_n):
         send(c_hbm, c_got.at[e * y_n], c_base + e * y_n, {"gy": peer(e, 0)})
+
+    for src, lo, hi, q in ((d_hbm, D_LO, D_HI, 0), (bg_hbm, B_LO, B_HI, 1)):
+        send(src.at[pl.ds(rows - OFF, OFF)], db_halo.at[0, q], lo, {"gx": gxo(1)})
+        send(src.at[pl.ds(0, OFF)], db_halo.at[1, q], hi, {"gx": gxo(-1)})
 
     loads[0].wait()
     pad_n[0:kx, :] = n_in[...]
@@ -181,11 +180,6 @@
     send(n_edge.at[1], n_halo.at[0], N_LO, {"gy": gyo(1)})
     send(n_edge.at[0], n_halo.at[1], N_HI, {"gy": gyo(-1)})
 
-    loads[1].wait()
-    loads[2].wait()
-    send(db_in.at[:, pl.ds(rows - OFF, OFF)], db_halo.at[0], DB_LO, {"gx": gxo(1)})
-    send(db_in.at[:, pl.ds(0, OFF)], db_halo.at[1], DB_HI, {"gx": gxo(-1)})
-
     def lead(a):
         at = pl.multiple_of(a * SUB, SUB)
         for r in range(SUB):
@@ -206,6 +200,9 @@
             send(own(0), own(rows), V_HI, {"gx": gxo(-1)})
         if k == 1:
             send(own(rows - HALO), own(-HALO), V_LO, {"gx": gxo(1)})
+
+    loads[1].wait()
+    loads[2].wait()
 
     def tile(t, i):
         return nat[t, pl.ds(pl.multiple_of((OFF + i) * SUB, SUB), SUB), :]
@@ -250,18 +247,6 @@
     send(strip.at[1, lo_rows], corner_hi.at[0], HL, {"gx": gxo(-1), "gy": gyo(1)})
     send(strip.at[0, lo_rows], corner_hi.at[1], HH, {"gx": gxo(-1), "gy": gyo(-1)})
 
-    for half in range(2):
-        for p in range(PLANES):
-            for ref, n in ((deal_own, 2 * LANES), (deal_side, LANES)):
-                k = lax.broadcasted_iota(jnp.int32, (n, LANES), 0)
-                l = lax.broadcasted_iota(jnp.int32, (n, LANES), 1) - half * HALF
-                if n == LANES:
-                    index = jnp.where(k < HALO, k, jnp.where(k < 2 * HALO, k + 2 * LANES, -1))
-                else:
-                    index = k + HALO
-                hit = (PLANES * l + p == index) & (l >= 0) & (l < HALF)
-                ref[half * n : (half + 1) * n, p * LANES : (p + 1) * LANES] = jnp.where(hit, 1.0, 0.0).astype(BF16)
-
     loads[6].wait()
     arrived(e_halo.at[0], E_LO)
     arrived(e_halo.at[1], E_HI)
@@ -297,6 +282,18 @@
         for e in range(1, x_n):
             send(eg.at[d], eg.at[e * y_n + d], e_base + e * y_n + d, {"gy": peer(e, 0)})
 
+    for half in range(2):
+        for p in range(PLANES):
+            for ref, n in ((deal_own, 2 * LANES), (deal_side, LANES)):
+                k = lax.broadcasted_iota(jnp.int32, (n, LANES), 0)
+                l = lax.broadcasted_iota(jnp.int32, (n, LANES), 1) - half * HALF
+                if n == LANES:
+                    index = jnp.where(k < HALO, k, jnp.where(k < 2 * HALO, k + 2 * LANES, -1))
+                else:
+                    index = k + HALO
+                hit = (PLANES * l + p == index) & (l >= 0) & (l < HALF)
+                ref[half * n : (half + 1) * n, p * LANES : (p + 1) * LANES] = jnp.where(hit, 1.0, 0.0).astype(BF16)
+
     one = jnp.float32(1.0)
     west_gain, east_gain = jnp.where(gy > 0, one, 0.0), jnp.where(gy < gy_n - 1, one, 0.0)
     low_gain, high_gain = jnp.where(gx > 0, one, 0.0), jnp.where(gx < gx_n - 1, one, 0.0)
@@ -316,44 +313,42 @@
     if rows % PER:
         own_sides(full, rows % PER)
 
-    arrived(own(-HALO), V_LO)
-    arrived(own(rows), V_HI)
+    def dealt(natural, firsts, count, apart):
+        def tiles(ts, shift):
+            return jnp.concatenate(
+                [jnp.concatenate([natural(t, pl.ds(f + shift, count)) for t in ts], axis=1) for f in firsts], axis=0
+            )
+
+        wide = jnp.concatenate([tiles((0, 1), 0), tiles((0, 1), apart)], axis=1)
+        sides = jnp.concatenate([tiles((2,), 0), tiles((2,), apart)], axis=1)
+        return fold(
+            jnp.dot(pieces(wide, 2), deal_own[...], preferred_element_type=F32)
+            + jnp.dot(pieces(sides, 2), deal_side[...], preferred_element_type=F32)
+        )
+
+    def deal_velocity(firsts, count):
+        out = dealt(
+            lambda t, at: nat[t, at, :] if t < 2 else side[at, :],
+            [f * SUB for f in firsts],
+            count * SUB,
+            half_rows * SUB,
+        )
+        for k, f in enumerate(firsts):
+            for u in range(count):
+                for p in range(PLANES):
+                    at = (k * count + u) * SUB
+                    vel[p, f + u] = out[at : at + SUB, p * LANES : (p + 1) * LANES]
+
+    wide_rows = vel.shape[1]
+    deal_velocity([OFF], half_rows)
+
+    for s in range(2):
+        for q in range(2):
+            arrived(db_halo.at[s, q], (D_LO, D_HI, B_LO, B_HI)[2 * q + s])
     for s, slot in ((0, LL), (1, LH)):
         arrived(corner_lo.at[s], slot)
     for s, slot in ((0, HL), (1, HH)):
         arrived(corner_hi.at[s], slot)
-    for i in range(HALO):
-        for corner, row, at, slab, gain in (
-            (corner_lo, rows - HALO + i, OFF - HALO + i, (rows - HALO + i) // PER - first_hi, low_gain),
-            (corner_hi, i, OFF + rows + i, 1 + i // PER, high_gain),
-        ):
-            here = slice(at * SUB, (at + 1) * SUB)
-            side[here, :] = unpack(corner[0, slab], corner[1, slab], row % PER) * gain
-            for t in range(2):
-                nat[t, here, :] = nat[t, here, :] * gain
-
-    def dealt(natural, first, count, apart):
-        near, far = pl.ds(first, count), pl.ds(first + apart, count)
-        wide = jnp.concatenate([natural(t, at) for at in (near, far) for t in range(2)], axis=1)
-        sides = jnp.concatenate([natural(2, at) for at in (near, far)], axis=1)
-        return fold(
-            jnp.dot(pieces(wide), deal_own[...], preferred_element_type=F32)
-            + jnp.dot(pieces(sides), deal_side[...], preferred_element_type=F32)
-        )
-
-    wide_rows = vel.shape[1]
-    chunk = 16
-
-    @pl.loop(0, wide_rows // chunk)
-    def _(c):
-        first = pl.multiple_of(c * chunk * SUB, chunk * SUB)
-        out = dealt(lambda t, at: nat[t, at, :] if t < 2 else side[at, :], first, chunk * SUB, half_rows * SUB)
-        for u in range(chunk):
-            for p in range(PLANES):
-                vel[p, c * chunk + u] = out[u * SUB : (u + 1) * SUB, p * LANES : (p + 1) * LANES]
-
-    for s, slot in ((0, DB_LO), (1, DB_HI)):
-        arrived(db_halo.at[s], slot)
     tiles = rows // SUB
     for b in range(tiles + 6):
         values = []
@@ -384,7 +379,7 @@
             g_nat[t, here, :] = keep * d * s * s
             b_nat[t, here, :] = keep / d
     for natural, out in ((g_nat, g_wide), (b_nat, b_wide)):
-        out[...] = dealt(lambda t, at, natural=natural: natural[t, at, :], 0, wide_rows, half_rows)
+        out[...] = dealt(lambda t, at, natural=natural: natural[t, at, :], [0], wide_rows, half_rows)
 
     for slot in range(y_n, gy_n):
         arrived(c_got.at[slot], c_base + slot)
@@ -410,7 +405,7 @@
     for b in range(gx_n):
         for t in range(3):
             n_all[b * kx : (b + 1) * kx, t * LANES : (t + 1) * LANES] = ng[b, t, 0:kx, :]
-    split = pieces(n_all[...])
+    split = pieces(n_all[...], 3)
     lower = jnp.dot(split[:, 0 : 2 * LANES], deal_own[0 : 2 * LANES, :], preferred_element_type=F32)
     lower += jnp.dot(split[:, 2 * LANES :], deal_side[0:LANES, :], preferred_element_type=F32)
     for p in range(PLANES):
@@ -420,12 +415,13 @@
             n_parts[j, 0:LANES, at] = part.astype(BF16)
             n_parts[j, LANES:, at] = roll(part, HALF).astype(BF16)
 
-    @pl.loop(0, wide_rows // chunk)
-    def _(c):
+    begin = OFF - HALO
+    chunk = half_rows // 2 + HALO
+    for c in range(2):
         n = chunk * SUB
-        near = pl.ds(pl.multiple_of(c * n, n), n)
-        far = pl.ds(pl.multiple_of(c * n + half_rows * SUB, SUB), n)
-        left = pieces(jnp.concatenate([panel[near, :], panel[far, :]], axis=1))
+        first = begin + c * chunk
+        near, far = (slice((first + a) * SUB, (first + a) * SUB + n) for a in (0, half_rows))
+        left = pieces(jnp.concatenate([panel[near, :], panel[far, :]], axis=1), 3)
         a = jnp.dot(left, n_parts[0], preferred_element_type=F32)
         b = jnp.dot(left[0 : 2 * n], n_parts[1], preferred_element_type=F32)
         field = a[0:n] + (
@@ -434,23 +430,37 @@
         )
         for p in range(PLANES):
             at = slice(p * LANES, (p + 1) * LANES)
-            first = pl.multiple_of(c * chunk, chunk)
-            g, w = g_wide[pl.ds(first, chunk), at], b_wide[pl.ds(first, chunk), at]
+            g, w = g_wide[first : first + chunk, at], b_wide[first : first + chunk, at]
             for u in range(chunk):
                 q = 1.0 + GAIN * jnp.tanh(field[u * SUB : (u + 1) * SUB, at])
-                mod[p, c * chunk + u] = jnp.broadcast_to(g[u : u + 1], (SUB, LANES)) * (q * q)
-                buoy[p, c * chunk + u] = jnp.broadcast_to(w[u : u + 1], (SUB, LANES))
+                mod[p, first + u] = jnp.broadcast_to(g[u : u + 1], (SUB, LANES)) * (q * q)
+                buoy[p, first + u] = jnp.broadcast_to(w[u : u + 1], (SUB, LANES))
+
+    arrived(own(-HALO), V_LO)
+    arrived(own(rows), V_HI)
+    for i in range(HALO):
+        for corner, row, at, slab, gain in (
+            (corner_lo, rows - HALO + i, OFF - HALO + i, (rows - HALO + i) // PER - first_hi, low_gain),
+            (corner_hi, i, OFF + rows + i, 1 + i // PER, high_gain),
+        ):
+            here = slice(at * SUB, (at + 1) * SUB)
+            side[here, :] = unpack(corner[0, slab], corner[1, slab], row % PER) * gain
+            for t in range(2):
+                nat[t, here, :] = nat[t, here, :] * gain
+
+    deal_velocity([0, OFF + half_rows], OFF)
 
     zero = jnp.zeros((SUB, LANES), F32)
     for step in range(1, STEPS + 1):
         begin = OFF - HALO + 3 * step - 2
         count = half_rows + 2 * HALO + 3 - 6 * step
-        chunks = -(-count // UNROLL)
-
-        def sweep(c, carry, begin=begin, first=step == 1):
+        unroll = min(range(11, 15), key=lambda n: -count % n)
+        chunks = -(-count // unroll)
+
+        def sweep(c, carry, begin=begin, unroll=unroll, first=step == 1):
             carry = list(carry)
-            for u in range(UNROLL):
-                i = begin + c * UNROLL + u
+            for u in range(unroll):
+                i = begin + c * unroll + u
                 v0 = [carry[p][1] for p in range(PLANES)]
                 n1_ = [carry[p][6] for p in range(PLANES)]
                 v0 += [roll(v0[0], -1), roll(v0[1], -1), roll(v0[-1], 1)]
@@ -482,27 +492,18 @@
         )
         lax.fori_loop(0, chunks, sweep, start)
 
-    @pl.loop(0, half_rows // SUB)
-    def _(a):
-        at = pl.multiple_of(a * SUB, SUB)
-        block = jnp.concatenate(
-            [
-                jnp.concatenate([peak[p, OFF + a * SUB + u] for u in range(SUB)], axis=0)
-                for p in range(PLANES)
-            ],
-            axis=1,
-        )
-        back = fold(
-            lax.dot_general(
-                pieces(block), deal_own[...], (((1,), (1,)), ((), ())), preferred_element_type=F32
-            )
-        )
-        for t in range(4):
-            flat[t] = back[:, t * LANES : (t + 1) * LANES]
-            upper = pl.multiple_of(at + (t // 2) * half_rows, SUB)
+    block = jnp.concatenate([peak[p, OFF : OFF + half_rows].reshape(half_rows * SUB, LANES) for p in range(PLANES)], axis=1)
+    back = fold(
+        lax.dot_general(pieces(block, 2), deal_own[...], (((1,), (1,)), ((), ())), preferred_element_type=F32)
+    )
+    for t in range(4):
+        flat[t] = back[:, t * LANES : (t + 1) * LANES]
+    for t in range(4):
+        for a in range(half_rows // SUB):
+            at = (t // 2) * half_rows + a * SUB
             for r in range(SUB):
-                out_ref[r, pl.ds(upper, SUB), (t % 2) * LANES : (t % 2 + 1) * LANES] = flat[
-                    t, pl.ds(r, SUB, stride=SUB), :
+                out_ref[r, at : at + SUB, (t % 2) * LANES : (t % 2 + 1) * LANES] = flat[
+                    t, pl.ds(a * SUB * SUB + r, SUB, stride=SUB), :
                 ]
 
     for copy in sent:
@@ -519,7 +520,7 @@
     slabs = -(-rows // PER)
     lo_len = 1 + (HALO - 1) // PER + 1
     hi_len = slabs - (rows - HALO) // PER + 1
-    sends = 4 + 2 + 2 + 2 + 4 + 2 * (gy_n - 1) + gx_n - 1
+    sends = 4 + 2 + 4 + 2 + 4 + 2 * (gy_n - 1) + gx_n - 1
     vmem = lambda *shape: pltpu.VMEM(shape, F32)
     scratch = [
         vmem(reals, rows, cols),
@@ -558,15 +559,15 @@
         vmem(PLANES, wide, SUB, LANES),
         vmem(PLANES, wide, SUB, LANES),
         vmem(PLANES, wide, SUB, LANES),
-        vmem(4, SUB * SUB, LANES),
+        vmem(4, rows // 2 * SUB, LANES),
         pltpu.SemaphoreType.DMA((8,)),
         pltpu.SemaphoreType.DMA((sends,)),
-        pltpu.SemaphoreType.DMA((14 + 2 * gy_n + gx_n,)),
+        pltpu.SemaphoreType.DMA((16 + 2 * gy_n + gx_n,)),
     ]
     return pl.pallas_call(
         functools.partial(kernel, (gx_n, gy_n, y_n, kx, ky)),
         out_shape=jax.ShapeDtypeStruct(initial_velocity.shape, F32),
-        in_specs=[pl.BlockSpec(memory_space=pl.ANY)] * 6,
+        in_specs=[pl.BlockSpec(memory_space=pltpu.HBM)] * 6,
         out_specs=pl.BlockSpec(memory_space=pltpu.VMEM),
         scratch_shapes=scratch,
         compiler_params=pltpu.CompilerParams(

time: 50.1 us -> 42.1 us (0.84)
  Pallas kernels: 48.1 us -> 40.1 us
    pallas_call x1, Pallas kernels: 48.1 us -> 40.1 us  [on_device(): pl.pallas_call(functools.partial(kernel, (gx_n, gy_n, y_n, kx, ky)), out_...]
where the time goes in v3:
time: 42.1 us; the launch traced here: 42 us
  Pallas kernels  40.1 us (95%)
  local copies, waits for them, and re-layouts  1.87 us (4%)
    pallas_call x1, Pallas kernels, on_device(): pl.pallas_call(functools.partial(kernel, (gx_n, gy_n, y_n, kx, ky)), out_...  40.1 us
    unnamed x1, local copies, waits for them, and re-layouts  1.87 us

profile of v3, /device:TPU:2, one launch (start us, length us, event | category | flops | bytes accessed | tf_op | source)
XLA Modules:
  0.0 42.0 jit_solution(13491154980062406832)
XLA Ops:
  0.0 40.1 %shard_map.64 = f32[8,64,256]{2,1,0:T(8,128)} custom-call(f32[8,64,256]{2,1,0:T(8,128)} %v_hbm.1, f32[64,256]{1,0:T(8,128)} %bg_hbm.1, f32[64,256]{1,0:T(8,128)} %d_hbm.1, f32[6,64]{1,0:T(8,128)} %bitcast.3, f32[12,256]{1,0:T(8,128)} %n_hbm.1, f32[6,8,96]{2,1,0:T(8,128)} %bitcast.2), custom_call_target="tpu_custom_call" | custom-call | tf_op jit(solution)/shard_map/pallas_call | solution.py:567
  40.1 1.9 %copy.8 = f32[8,64,256]{2,1,0:T(8,128)} copy(f32[8,64,256]{2,1,0:T(8,128)} %shard_map.64) | data formatting | bytes 1048576

commit v4 on v3

--- a/solution.py
+++ b/solution.py
@@ -45,7 +45,7 @@
     return x[0:n] + x[n:]
 
 
-E_LO, E_HI, N_LO, N_HI, V_LO, V_HI, D_LO, D_HI, B_LO, B_HI, S_LO, S_HI, LL, LH, HL, HH = range(16)
+N_LO, N_HI, V_LO, V_HI, D_LO, D_HI, B_LO, B_HI, S_LO, S_HI, LL, LH, HL, HH = range(14)
 
 
 def kernel(
@@ -59,7 +59,6 @@
     out_ref,
     v_in,
     db_in,
-    e_in,
     n_in,
     pad_e,
     pad_n,
@@ -70,7 +69,7 @@
     ng,
     n_all,
     n_parts,
-    e_halo,
+    e_got,
     n_edge,
     n_halo,
     nat,
@@ -120,22 +119,40 @@
     bands = ((0, OFF), (rows - OFF, OFF), (OFF, mid_rows))
     moves = [(n_hbm, n_in), (d_hbm, db_in.at[0]), (bg_hbm, db_in.at[1])]
     moves += [(v_hbm.at[:, pl.ds(a, n)], v_in.at[:, pl.ds(a, n)]) for a, n in bands]
-    moves += [(e_hbm, e_in), (c_hbm, c_got.at[0])]
+    moves += [(e_hbm, e_got.at[1, 0]), (c_hbm, c_got.at[0])]
     loads = [pltpu.make_async_copy(src, dst, load_sem.at[i]) for i, (src, dst) in enumerate(moves)]
     for load in loads:
         load.start()
 
-    partners = [{"gx": gxo(a), "gy": gyo(b)} for a in (-1, 0, 1) for b in (-1, 0, 1) if a or b]
-    partners += [{"gy": peer(0, d)} for d in range(1, y_n)]
-    partners += [{"gy": peer(e, 0)} for e in range(1, x_n)]
-    partners += [{"gx": gxo(o)} for o in range(1, gx_n)]
+    in_x = {-1: gx > 0, 0: None, 1: gx < gx_n - 1}
+    in_y = {-1: gy > 0, 0: None, 1: gy < gy_n - 1}
+
+    def inside(a, b):
+        conditions = [c for c in (in_x[a], in_y[b]) if c is not None]
+        return functools.reduce(jnp.logical_and, conditions) if conditions else None
+
+    def under(condition, act):
+        if condition is None:
+            act()
+        else:
+            pl.when(condition)(act)
+
+    partners = [({"gx": gxo(a), "gy": gyo(b)}, inside(a, b)) for a in (-1, 0, 1) for b in (-1, 0, 1) if a or b]
+    partners += [({"gx": gxo(a), "gy": peer(0, d)}, in_x[a]) for a in (-1, 0, 1) for d in range(1, y_n)]
+    partners += [({"gy": peer(e, 0)}, None) for e in range(1, x_n)]
+    partners += [({"gx": gxo(o)}, None) for o in range(1, gx_n)]
     barrier = pltpu.get_barrier_semaphore()
-    for partner in partners:
-        pl.semaphore_signal(barrier, inc=1, device_id=partner, device_id_type=MESH)
+    expected = jnp.int32(0)
+    for partner, condition in partners:
+        under(
+            condition,
+            lambda partner=partner: pl.semaphore_signal(barrier, inc=1, device_id=partner, device_id_type=MESH),
+        )
+        expected += 1 if condition is None else jnp.where(condition, 1, 0)
 
     sent = []
 
-    def send(src, dst, slot, target):
+    def send(src, dst, slot, target, condition=None):
         copy = pltpu.make_async_remote_copy(
             src_ref=src,
             dst_ref=dst,
@@ -144,13 +161,19 @@
             device_id=target,
             device_id_type=MESH,
         )
-        copy.start()
-        sent.append(copy)
-
-    def arrived(dst, slot):
-        pltpu.make_async_copy(dst, dst, recv_sem.at[slot]).wait()
-
-    c_base = 16
+        under(condition, copy.start)
+        sent.append((copy, condition))
+
+    def arrived(dst, slot, condition=None):
+        under(condition, pltpu.make_async_copy(dst, dst, recv_sem.at[slot]).wait)
+        if condition is not None:
+
+            @pl.when(jnp.logical_not(condition))
+            def _():
+                dst[...] = jnp.zeros(dst.shape, dst.dtype)
+
+    z_base = 14
+    c_base = z_base + 3 * y_n
     e_base = c_base + gy_n
     n_base = e_base + gy_n
 
@@ -159,26 +182,28 @@
     e_all[...] = jnp.zeros_like(e_all)
     n_all[...] = jnp.zeros_like(n_all)
 
-    pl.semaphore_wait(barrier, len(partners))
-
-    send(e_hbm, e_halo.at[0], E_LO, {"gx": gxo(1)})
-    send(e_hbm, e_halo.at[1], E_HI, {"gx": gxo(-1)})
+    pl.semaphore_wait(barrier, expected)
+
+    for d in range(y_n):
+        for a in (0, 1, -1) if d else (1, -1):
+            slot = z_base + (1 - a) * y_n + d
+            send(e_hbm, e_got.at[1 - a, d], slot, {"gx": gxo(a), "gy": peer(0, d)}, in_x[a])
     for d in range(1, y_n):
         send(c_hbm, c_got.at[d], c_base + d, {"gy": peer(0, d)})
     for e in range(1, x_n):
         send(c_hbm, c_got.at[e * y_n], c_base + e * y_n, {"gy": peer(e, 0)})
 
     for src, lo, hi, q in ((d_hbm, D_LO, D_HI, 0), (bg_hbm, B_LO, B_HI, 1)):
-        send(src.at[pl.ds(rows - OFF, OFF)], db_halo.at[0, q], lo, {"gx": gxo(1)})
-        send(src.at[pl.ds(0, OFF)], db_halo.at[1, q], hi, {"gx": gxo(-1)})
+        send(src.at[pl.ds(rows - OFF, OFF)], db_halo.at[0, q], lo, {"gx": gxo(1)}, in_x[1])
+        send(src.at[pl.ds(0, OFF)], db_halo.at[1, q], hi, {"gx": gxo(-1)}, in_x[-1])
 
     loads[0].wait()
     pad_n[0:kx, :] = n_in[...]
     n0, n1 = (pad_n[0:SUB, 0:LANES], pad_n[0:SUB, LANES:]), (pad_n[SUB:, 0:LANES], pad_n[SUB:, LANES:])
     n_edge[0] = jnp.where(lane < HALO, n0[0], roll(n1[0], HALO))
     n_edge[1] = jnp.where(lane < HALO, roll(n0[1], HALO), roll(n1[1], 2 * HALO))
-    send(n_edge.at[1], n_halo.at[0], N_LO, {"gy": gyo(1)})
-    send(n_edge.at[0], n_halo.at[1], N_HI, {"gy": gyo(-1)})
+    send(n_edge.at[1], n_halo.at[0], N_LO, {"gy": gyo(1)}, in_y[1])
+    send(n_edge.at[0], n_halo.at[1], N_HI, {"gy": gyo(-1)}, in_y[-1])
 
     def lead(a):
         at = pl.multiple_of(a * SUB, SUB)
@@ -197,9 +222,9 @@
         loads[3 + k].wait()
         pl.loop(first // SUB, (first + count) // SUB)(lead)
         if k == 0:
-            send(own(0), own(rows), V_HI, {"gx": gxo(-1)})
+            send(own(0), own(rows), V_HI, {"gx": gxo(-1)}, in_x[-1])
         if k == 1:
-            send(own(rows - HALO), own(-HALO), V_LO, {"gx": gxo(1)})
+            send(own(rows - HALO), own(-HALO), V_LO, {"gx": gxo(1)}, in_x[1])
 
     loads[1].wait()
     loads[2].wait()
@@ -240,29 +265,33 @@
     first_hi = (rows - HALO) // PER
     lo_len, hi_len = corner_hi.shape[1], corner_lo.shape[1]
     lo_rows, hi_rows = pl.ds(0, lo_len), pl.ds(1 + first_hi, hi_len)
-    send(strip.at[1], strip_halo.at[0], S_LO, {"gy": gyo(1)})
-    send(strip.at[0], strip_halo.at[1], S_HI, {"gy": gyo(-1)})
-    send(strip.at[1, hi_rows], corner_lo.at[0], LL, {"gx": gxo(1), "gy": gyo(1)})
-    send(strip.at[0, hi_rows], corner_lo.at[1], LH, {"gx": gxo(1), "gy": gyo(-1)})
-    send(strip.at[1, lo_rows], corner_hi.at[0], HL, {"gx": gxo(-1), "gy": gyo(1)})
-    send(strip.at[0, lo_rows], corner_hi.at[1], HH, {"gx": gxo(-1), "gy": gyo(-1)})
+    send(strip.at[1], strip_halo.at[0], S_LO, {"gy": gyo(1)}, in_y[1])
+    send(strip.at[0], strip_halo.at[1], S_HI, {"gy": gyo(-1)}, in_y[-1])
+    send(strip.at[1, hi_rows], corner_lo.at[0], LL, {"gx": gxo(1), "gy": gyo(1)}, inside(1, 1))
+    send(strip.at[0, hi_rows], corner_lo.at[1], LH, {"gx": gxo(1), "gy": gyo(-1)}, inside(1, -1))
+    send(strip.at[1, lo_rows], corner_hi.at[0], HL, {"gx": gxo(-1), "gy": gyo(1)}, inside(-1, 1))
+    send(strip.at[0, lo_rows], corner_hi.at[1], HH, {"gx": gxo(-1), "gy": gyo(-1)}, inside(-1, -1))
 
     loads[6].wait()
-    arrived(e_halo.at[0], E_LO)
-    arrived(e_halo.at[1], E_HI)
-    for k, piece in enumerate((e_halo[0], e_in[...], e_halo[1])):
-        pad_e[k, 0:ky, 0:rows] = piece
-    eg[0] = jnp.where(
-        lane < OFF,
-        roll(pad_e[0], OFF - rows),
-        jnp.where(lane < OFF + rows, roll(pad_e[1], OFF), roll(pad_e[2], OFF + rows)),
-    )
-    for d in range(1, y_n):
-        send(eg.at[0], eg.at[d], e_base + d, {"gy": peer(0, d)})
-    for e in range(1, x_n):
-        send(eg.at[0], eg.at[e * y_n], e_base + e * y_n, {"gy": peer(e, 0)})
-    arrived(n_halo.at[0], N_LO)
-    arrived(n_halo.at[1], N_HI)
+    for d in sorted(range(y_n), key=lambda d: min(d, y_n - d)):
+        if d:
+            arrived(c_got.at[d], c_base + d)
+            for e in range(1, x_n):
+                send(c_got.at[d], c_got.at[e * y_n + d], c_base + e * y_n + d, {"gy": peer(e, 0)})
+        for k in range(3):
+            if k != 1 or d:
+                arrived(e_got.at[k, d], z_base + k * y_n + d, in_x[k - 1])
+            pad_e[k, 0:ky, 0:rows] = e_got[k, d]
+        eg[d] = jnp.where(
+            lane < OFF,
+            roll(pad_e[0], OFF - rows),
+            jnp.where(lane < OFF + rows, roll(pad_e[1], OFF), roll(pad_e[2], OFF + rows)),
+        )
+        for e in range(1, x_n):
+            send(eg.at[d], eg.at[e * y_n + d], e_base + e * y_n + d, {"gy": peer(e, 0)})
+
+    arrived(n_halo.at[0], N_LO, in_y[-1])
+    arrived(n_halo.at[1], N_HI, in_y[1])
 
     def flank(west, east):
         return jnp.where(lane < HALO, west, jnp.where(lane < 2 * HALO, east, 0.0))
@@ -273,14 +302,6 @@
             ng[gx, t, half * SUB : (half + 1) * SUB, :] = value
     for o in range(1, gx_n):
         send(ng.at[gx], ng.at[gx], n_base + o, {"gx": gxo(o)})
-
-    for d in sorted(range(1, y_n), key=lambda d: min(d, y_n - d)):
-        arrived(c_got.at[d], c_base + d)
-        for e in range(1, x_n):
-            send(c_got.at[d], c_got.at[e * y_n + d], c_base + e * y_n + d, {"gy": peer(e, 0)})
-        arrived(eg.at[d], e_base + d)
-        for e in range(1, x_n):
-            send(eg.at[d], eg.at[e * y_n + d], e_base + e * y_n + d, {"gy": peer(e, 0)})
 
     for half in range(2):
         for p in range(PLANES):
@@ -294,61 +315,81 @@
                 hit = (PLANES * l + p == index) & (l >= 0) & (l < HALF)
                 ref[half * n : (half + 1) * n, p * LANES : (p + 1) * LANES] = jnp.where(hit, 1.0, 0.0).astype(BF16)
 
-    one = jnp.float32(1.0)
-    west_gain, east_gain = jnp.where(gy > 0, one, 0.0), jnp.where(gy < gy_n - 1, one, 0.0)
-    low_gain, high_gain = jnp.where(gx > 0, one, 0.0), jnp.where(gx < gx_n - 1, one, 0.0)
-
-    arrived(strip_halo.at[0], S_LO)
-    arrived(strip_halo.at[1], S_HI)
-
-    def unpack(west, east, p):
-        return flank(roll(west, -p * HALO) * west_gain, roll(east, (1 - p) * HALO) * east_gain)
-
-    def own_sides(g, count):
-        for p in range(count):
-            at = pl.multiple_of((OFF + g * PER + p) * SUB, SUB)
-            side[pl.ds(at, SUB), :] = unpack(strip_halo[0, 1 + g], strip_halo[1, 1 + g], p)
-
-    pl.loop(0, full)(lambda g: own_sides(g, PER))
-    if rows % PER:
-        own_sides(full, rows % PER)
-
-    def dealt(natural, firsts, count, apart):
+    def dealt(natural, firsts, count, apart, middle, beside):
         def tiles(ts, shift):
             return jnp.concatenate(
                 [jnp.concatenate([natural(t, pl.ds(f + shift, count)) for t in ts], axis=1) for f in firsts], axis=0
             )
 
-        wide = jnp.concatenate([tiles((0, 1), 0), tiles((0, 1), apart)], axis=1)
-        sides = jnp.concatenate([tiles((2,), 0), tiles((2,), apart)], axis=1)
-        return fold(
-            jnp.dot(pieces(wide, 2), deal_own[...], preferred_element_type=F32)
-            + jnp.dot(pieces(sides, 2), deal_side[...], preferred_element_type=F32)
-        )
-
-    def deal_velocity(firsts, count):
+        total = None
+        for wanted, ts, deal in ((middle, (0, 1), deal_own), (beside, (2,), deal_side)):
+            if wanted:
+                left = pieces(jnp.concatenate([tiles(ts, 0), tiles(ts, apart)], axis=1), 2)
+                term = jnp.dot(left, deal[...], preferred_element_type=F32)
+                total = term if total is None else total + term
+        return fold(total)
+
+    def deal_velocity(firsts, count, middle, beside):
         out = dealt(
             lambda t, at: nat[t, at, :] if t < 2 else side[at, :],
             [f * SUB for f in firsts],
             count * SUB,
             half_rows * SUB,
+            middle,
+            beside,
         )
         for k, f in enumerate(firsts):
             for u in range(count):
                 for p in range(PLANES):
                     at = (k * count + u) * SUB
-                    vel[p, f + u] = out[at : at + SUB, p * LANES : (p + 1) * LANES]
+                    value = out[at : at + SUB, p * LANES : (p + 1) * LANES]
+                    vel[p, f + u] = value if middle else vel[p, f + u] + value
 
     wide_rows = vel.shape[1]
-    deal_velocity([OFF], half_rows)
-
+    deal_velocity([OFF], half_rows, True, False)
+
+    for slot in range(y_n, gy_n):
+        arrived(c_got.at[slot], c_base + slot)
+        arrived(eg.at[slot], e_base + slot)
+    loads[7].wait()
+    c_all[...] = jnp.zeros_like(c_all)
+    for slot in range(gy_n):
+        e_all[slot * ky : (slot + 1) * ky, :] = eg[slot, 0:ky, :]
+        for k in range(ky):
+            at = (slot * ky + k) * SUB
+            c_all[at : at + SUB, 0 : c_got.shape[3]] = c_got[slot, k]
+    nat_rows = OFF + rows + OFF
+    lhs = jnp.transpose(e_all[...])[0:nat_rows, 0:modes]
+    for r in range(SUB):
+        rhs = c_all[pl.ds(r, modes, stride=SUB), :]
+        panel[pl.ds(r, nat_rows, stride=SUB), :] = jnp.dot(
+            lhs, rhs, precision=lax.Precision.HIGHEST, preferred_element_type=F32
+        )
+
+    for o in range(1, gx_n):
+        at = gxo(-o)
+        arrived(ng.at[at], n_base + o)
+    for b in range(gx_n):
+        for t in range(3):
+            n_all[b * kx : (b + 1) * kx, t * LANES : (t + 1) * LANES] = ng[b, t, 0:kx, :]
+    split = pieces(n_all[...], 3)
+    lower = jnp.dot(split[:, 0 : 2 * LANES], deal_own[0 : 2 * LANES, :], preferred_element_type=F32)
+    lower += jnp.dot(split[:, 2 * LANES :], deal_side[0:LANES, :], preferred_element_type=F32)
+    for p in range(PLANES):
+        at = slice(p * LANES, (p + 1) * LANES)
+        for j in range(3):
+            part = lower[j * LANES : (j + 1) * LANES, at]
+            n_parts[j, 0:LANES, at] = part.astype(BF16)
+            n_parts[j, LANES:, at] = roll(part, HALF).astype(BF16)
+
+    arrived(strip_halo.at[0], S_LO, in_y[-1])
+    arrived(strip_halo.at[1], S_HI, in_y[1])
     for s in range(2):
         for q in range(2):
-            arrived(db_halo.at[s, q], (D_LO, D_HI, B_LO, B_HI)[2 * q + s])
-    for s, slot in ((0, LL), (1, LH)):
-        arrived(corner_lo.at[s], slot)
-    for s, slot in ((0, HL), (1, HH)):
-        arrived(corner_hi.at[s], slot)
+            arrived(db_halo.at[s, q], (D_LO, D_HI, B_LO, B_HI)[2 * q + s], in_x[2 * s - 1])
+    for s in range(2):
+        arrived(corner_lo.at[s], (LL, LH)[s], inside(-1, 2 * s - 1))
+        arrived(corner_hi.at[s], (HL, HH)[s], inside(1, 2 * s - 1))
     tiles = rows // SUB
     for b in range(tiles + 6):
         values = []
@@ -368,52 +409,13 @@
                 p = 2 * a + q
             t0, t1 = (body[a * SUB : (a + 1) * SUB, t * LANES : (t + 1) * LANES] for t in range(2))
             values.append((t0, t1, flank(roll(w, -p * HALO), roll(e, (1 - p) * HALO))))
-        gain = low_gain if b < 3 else high_gain if b >= tiles + 3 else one
         here = slice(b * SUB, (b + 1) * SUB)
         for t in range(3):
             d, s = values[0][t], values[1][t]
-            keep = SCALE * gain
-            if t == 2:
-                keep = jnp.where(lane < HALO, west_gain, east_gain) * keep
-                d = jnp.where(lane < 2 * HALO, d, 1.0)
-            g_nat[t, here, :] = keep * d * s * s
-            b_nat[t, here, :] = keep / d
+            g_nat[t, here, :] = SCALE * d * s * s
+            b_nat[t, here, :] = jnp.where(d > 0.0, SCALE / jnp.where(d > 0.0, d, 1.0), 0.0)
     for natural, out in ((g_nat, g_wide), (b_nat, b_wide)):
-        out[...] = dealt(lambda t, at, natural=natural: natural[t, at, :], [0], wide_rows, half_rows)
-
-    for slot in range(y_n, gy_n):
-        arrived(c_got.at[slot], c_base + slot)
-        arrived(eg.at[slot], e_base + slot)
-    loads[7].wait()
-    c_all[...] = jnp.zeros_like(c_all)
-    for slot in range(gy_n):
-        e_all[slot * ky : (slot + 1) * ky, :] = eg[slot, 0:ky, :]
-        for k in range(ky):
-            at = (slot * ky + k) * SUB
-            c_all[at : at + SUB, 0 : c_got.shape[3]] = c_got[slot, k]
-    nat_rows = OFF + rows + OFF
-    lhs = jnp.transpose(e_all[...])[0:nat_rows, 0:modes]
-    for r in range(SUB):
-        rhs = c_all[pl.ds(r, modes, stride=SUB), :]
-        panel[pl.ds(r, nat_rows, stride=SUB), :] = jnp.dot(
-            lhs, rhs, precision=lax.Precision.HIGHEST, preferred_element_type=F32
-        )
-
-    for o in range(1, gx_n):
-        at = gxo(-o)
-        arrived(ng.at[at], n_base + o)
-    for b in range(gx_n):
-        for t in range(3):
-            n_all[b * kx : (b + 1) * kx, t * LANES : (t + 1) * LANES] = ng[b, t, 0:kx, :]
-    split = pieces(n_all[...], 3)
-    lower = jnp.dot(split[:, 0 : 2 * LANES], deal_own[0 : 2 * LANES, :], preferred_element_type=F32)
-    lower += jnp.dot(split[:, 2 * LANES :], deal_side[0:LANES, :], preferred_element_type=F32)
-    for p in range(PLANES):
-        at = slice(p * LANES, (p + 1) * LANES)
-        for j in range(3):
-            part = lower[j * LANES : (j + 1) * LANES, at]
-            n_parts[j, 0:LANES, at] = part.astype(BF16)
-            n_parts[j, LANES:, at] = roll(part, HALF).astype(BF16)
+        out[...] = dealt(lambda t, at, natural=natural: natural[t, at, :], [0], wide_rows, half_rows, True, True)
 
     begin = OFF - HALO
     chunk = half_rows // 2 + HALO
@@ -436,19 +438,28 @@
                 mod[p, first + u] = jnp.broadcast_to(g[u : u + 1], (SUB, LANES)) * (q * q)
                 buoy[p, first + u] = jnp.broadcast_to(w[u : u + 1], (SUB, LANES))
 
-    arrived(own(-HALO), V_LO)
-    arrived(own(rows), V_HI)
+    def unpack(west, east, p):
+        return flank(roll(west, -p * HALO), roll(east, (1 - p) * HALO))
+
+    def own_sides(g, count):
+        for p in range(count):
+            at = pl.multiple_of((OFF + g * PER + p) * SUB, SUB)
+            side[pl.ds(at, SUB), :] = unpack(strip_halo[0, 1 + g], strip_halo[1, 1 + g], p)
+
+    pl.loop(0, full)(lambda g: own_sides(g, PER))
+    if rows % PER:
+        own_sides(full, rows % PER)
+    deal_velocity([OFF], half_rows, False, True)
+
+    arrived(own(-HALO), V_LO, in_x[-1])
+    arrived(own(rows), V_HI, in_x[1])
     for i in range(HALO):
-        for corner, row, at, slab, gain in (
-            (corner_lo, rows - HALO + i, OFF - HALO + i, (rows - HALO + i) // PER - first_hi, low_gain),
-            (corner_hi, i, OFF + rows + i, 1 + i // PER, high_gain),
+        for corner, row, at, slab in (
+            (corner_lo, rows - HALO + i, OFF - HALO + i, (rows - HALO + i) // PER - first_hi),
+            (corner_hi, i, OFF + rows + i, 1 + i // PER),
         ):
-            here = slice(at * SUB, (at + 1) * SUB)
-            side[here, :] = unpack(corner[0, slab], corner[1, slab], row % PER) * gain
-            for t in range(2):
-                nat[t, here, :] = nat[t, here, :] * gain
-
-    deal_velocity([0, OFF + half_rows], OFF)
+            side[at * SUB : (at + 1) * SUB, :] = unpack(corner[0, slab], corner[1, slab], row % PER)
+    deal_velocity([0, OFF + half_rows], OFF, True, True)
 
     zero = jnp.zeros((SUB, LANES), F32)
     for step in range(1, STEPS + 1):
@@ -506,8 +517,8 @@
                     t, pl.ds(a * SUB * SUB + r, SUB, stride=SUB), :
                 ]
 
-    for copy in sent:
-        copy.wait_send()
+    for copy, condition in sent:
+        under(condition, copy.wait_send)
 
 
 def on_device(gx_n, gy_n, initial_velocity, background_speed, density, east_modes, north_modes, mode_coef):
@@ -520,12 +531,11 @@
     slabs = -(-rows // PER)
     lo_len = 1 + (HALO - 1) // PER + 1
     hi_len = slabs - (rows - HALO) // PER + 1
-    sends = 4 + 2 + 4 + 2 + 4 + 2 * (gy_n - 1) + gx_n - 1
+    sends = 14 + (3 * y_n - 1) + (gy_n - 1) + (x_n - 1) * y_n + gx_n - 1
     vmem = lambda *shape: pltpu.VMEM(shape, F32)
     scratch = [
         vmem(reals, rows, cols),
         vmem(2, rows, cols),
-        vmem(ky, rows),
         vmem(kx, cols),
         vmem(3, SUB, LANES),
         vmem(16, cols),
@@ -536,7 +546,7 @@
         vmem(gx_n, 3, 16, LANES),
         vmem(LANES, 3 * LANES),
         pltpu.VMEM((3, 2 * LANES, WIDE), BF16),
-        vmem(2, ky, rows),
+        vmem(3, y_n, ky, rows),
         vmem(2, SUB, LANES),
         vmem(2, SUB, LANES),
         vmem(2, natural * SUB, LANES),
@@ -562,7 +572,7 @@
         vmem(4, rows // 2 * SUB, LANES),
         pltpu.SemaphoreType.DMA((8,)),
         pltpu.SemaphoreType.DMA((sends,)),
-        pltpu.SemaphoreType.DMA((16 + 2 * gy_n + gx_n,)),
+        pltpu.SemaphoreType.DMA((14 + 3 * y_n + 2 * gy_n + gx_n,)),
     ]
     return pl.pallas_call(
         functools.partial(kernel, (gx_n, gy_n, y_n, kx, ky)),

time: 42.1 us -> 41.3 us (0.981)
  the two profiles are of different devices: /device:TPU:2 before, /device:TPU:31 now
where the time goes in v4:
time: 41.3 us; the launch traced here: 41.2 us
  Pallas kernels  39.3 us (95%)
  local copies, waits for them, and re-layouts  1.87 us (5%)
    pallas_call x1, Pallas kernels, on_device(): pl.pallas_call(functools.partial(kernel, (gx_n, gy_n, y_n, kx, ky)), out_...  39.3 us
    unnamed x1, local copies, waits for them, and re-layouts  1.87 us

profile of v4, /device:TPU:31, one launch (start us, length us, event | category | flops | bytes accessed | tf_op | source)
XLA Modules:
  0.0 41.2 jit_solution(6339658036364778037)
XLA Ops:
  0.0 39.3 %shard_map.64 = f32[8,64,256]{2,1,0:T(8,128)} custom-call(f32[8,64,256]{2,1,0:T(8,128)} %v_hbm.1, f32[64,256]{1,0:T(8,128)} %bg_hbm.1, f32[64,256]{1,0:T(8,128)} %d_hbm.1, f32[6,64]{1,0:T(8,128)} %bitcast.3, f32[12,256]{1,0:T(8,128)} %n_hbm.1, f32[6,8,96]{2,1,0:T(8,128)} %bitcast.2), custom_call_target="tpu_custom_call" | custom-call | tf_op jit(solution)/shard_map/pallas_call | solution.py:577
  39.3 1.9 %copy.8 = f32[8,64,256]{2,1,0:T(8,128)} copy(f32[8,64,256]{2,1,0:T(8,128)} %shard_map.64) | data formatting | bytes 1048576
